TPU v7x, 32 devices: a whole 2x2x4 slice. The times are simulated.
32 devices in a mesh: fsdp: 8 (over z, x), dp: 4 (over y, core).
Axes of the slice: x: 2, y: 2, z: 4, core: 2. Of those that a mesh axis runs over, the one named last changes fastest.
Arguments:
- patches: bfloat16 [160, 197, 768], P(('fsdp', 'dp')), may hold values from -6 to 6
- keep: int32 [160, 197], P(('fsdp', 'dp')), may hold values from -1 to 196, as said below
- ln1_gain: bfloat16 [768], P('fsdp'), may hold values from 0.5 to 1.5
- ln1_bias: bfloat16 [768], P('fsdp'), may hold values from -1.1953125 to 1.1953125
- w_qkv: bfloat16 [768, 2304], P('fsdp'), may hold values from -0.21875 to 0.21875
- b_query: bfloat16 [768], P('fsdp'), may hold values from -1.1953125 to 1.1953125
- b_value: bfloat16 [768], P('fsdp'), may hold values from -1.1953125 to 1.1953125
- w_out: bfloat16 [768, 768], P('fsdp'), may hold values from -1.75 to 1.75
- b_out: bfloat16 [768], P('fsdp'), may hold values from -1.1953125 to 1.1953125
- ln2_gain: bfloat16 [768], P('fsdp'), may hold values from 0.5 to 1.5
- ln2_bias: bfloat16 [768], P('fsdp'), may hold values from -1.1953125 to 1.1953125
- w_up: bfloat16 [768, 3072], P('fsdp'), may hold values from -0.21875 to 0.21875
- b_up: bfloat16 [3072], P('fsdp'), may hold values from -1.1953125 to 1.1953125
- w_down: bfloat16 [3072, 768], P('fsdp'), may hold values from -0.109375 to 0.109375
- b_down: bfloat16 [768], P('fsdp'), may hold values from -1.1953125 to 1.1953125
- cotangent: bfloat16 [160, 197, 768], P(('fsdp', 'dp')), may hold values from -6 to 6
Outputs:
- out_tokens: bfloat16 [160, 197, 768], P(('fsdp', 'dp'))
- grad_patches: float32 [160, 197, 768], P(('fsdp', 'dp'))
- g_ln1_gain: float32 [768], P('fsdp')
- g_ln1_bias: float32 [768], P('fsdp')
- g_w_qkv: float32 [768, 2304], P('fsdp')
- g_b_query: float32 [768], P('fsdp')
- g_b_value: float32 [768], P('fsdp')
- g_w_out: float32 [768, 768], P('fsdp')
- g_b_out: float32 [768], P('fsdp')
- g_ln2_gain: float32 [768], P('fsdp')
- g_ln2_bias: float32 [768], P('fsdp')
- g_w_up: float32 [768, 3072], P('fsdp')
- g_b_up: float32 [3072], P('fsdp')
- g_w_down: float32 [3072, 768], P('fsdp')
- g_b_down: float32 [768], P('fsdp')
Inputs may be any that keep to these rules, and one draw needn't show every extreme that they name: `keep`: each row holds the class token 0 first, then that image's kept patch positions in rising order, then -1 in the remaining slots. Every image keeps 197 // 4 or more positions, and some image keeps all 197.
All inputs are finite; a program needn't handle non-finite values.
Results may differ from a plain program's by a relative error of at most 0.018.
Values may be sent and summed in bfloat16 or wider, within the bound.
A program may use at most 192 MiB of HBM per device.

v0:
```python
import functools
import math

import jax
import jax.numpy as jnp
from jax import lax
from jax.experimental import pallas as pl
from jax.experimental.pallas import tpu as pltpu
from jax.sharding import PartitionSpec as P

H = 12
HD = 64
EPSILON = 1e-06
F32 = jnp.float32
BF16 = jnp.bfloat16
SLOT = 200
ROWS = 1024
BLOCK = 128
TILE = 256
NT = (((1,), (1,)), ((), ()))


def dot(left, right):
    return jnp.dot(left, right, preferred_element_type=F32)


def dot_nt(left, right):
    return lax.dot_general(left, right, NT, preferred_element_type=F32)


def tile_at(index, size):
    if isinstance(index, int):
        return pl.ds(index * size, size)
    return pl.ds(pl.multiple_of(index * size, size), size)


def loop(begin, end, body, unroll):
    if (end - begin) == unroll:
        for j in range(begin, end):
            body(j, 0)
        return

    def group(t, _):
        for u in range(unroll):
            body(begin + t * unroll + u, 0)
        return 0

    lax.fori_loop(0, (end - begin) // unroll, group, 0)


def norm_parts(values):
    centre = values - jnp.mean(values, axis=-1, keepdims=True)
    spread = jnp.mean(centre * centre, axis=-1, keepdims=True)
    inverse = lax.rsqrt(spread + EPSILON)
    return centre * inverse, inverse


def norm_back(hat, inverse, gain, grad):
    scaled = grad * gain
    along = jnp.mean(scaled * hat, axis=-1, keepdims=True)
    return inverse * (scaled - jnp.mean(scaled, axis=-1, keepdims=True) - hat * along)


def gelu_parts(hidden):
    size = jnp.abs(hidden)
    bell = jnp.exp(hidden * hidden * -0.5)
    t = 1.0 / (1.0 + size * (0.3275911 / math.sqrt(2.0)))
    tail = 1.061405429 * 0.5
    for term in (-1.453152027, 1.421413741, -0.284496736, 0.254829592):
        tail = tail * t + term * 0.5
    tail = tail * t * bell
    below = jnp.where(hidden >= 0, 1.0 - tail, tail)
    slope = below + hidden * (bell * (1.0 / math.sqrt(2.0 * math.pi)))
    return hidden * below, slope


def first_lanes(rows):
    return lax.broadcasted_iota(jnp.int32, (rows, 2 * HD), 1) < HD


def stage_gather(images, slots, patches, keep, stack, live, mask, token):
    stack[...] = jnp.zeros_like(stack)
    live[...] = jnp.zeros_like(live)

    def gather(i, _):
        row = keep[i]
        column = jnp.broadcast_to(row, (SLOT, SLOT)).T
        mask[i] = jnp.where(column >= 0, 0.0, -1e30)
        alive = (column >= 0).astype(F32)
        chosen = (column[:, :slots] == lax.broadcasted_iota(jnp.int32, (SLOT, slots), 1)).astype(F32).astype(BF16)
        rows = pl.ds(pl.multiple_of(i * SLOT, 8), SLOT)
        stack[rows, :] = dot(chosen, patches[i])
        live[rows, :] = alive[:, :BLOCK]
        return 0

    loop(0, images, gather, 1)

    def narrow(b, _):
        rows = tile_at(b, BLOCK)
        token[rows, :] = stack[rows, :].astype(BF16)
        return 0

    loop(0, ROWS // BLOCK, narrow, 2)


def stage_norm(gain, shift, token, normed, normed_t):
    def norm(b, _):
        rows = tile_at(b, BLOCK)
        hat, _ = norm_parts(token[rows, :].astype(F32))
        low = (hat * gain + shift).astype(BF16)
        normed[rows, :] = low
        normed_t[:, rows] = low.T
        return 0

    loop(0, ROWS // BLOCK, norm, 4)


def stage_grads(images, slots, width, cot, stack, live, dm, dm_t):
    stack[...] = jnp.zeros_like(stack)
    for i in range(images):
        stack[i * SLOT : i * SLOT + slots, :] = cot[i].astype(F32)

    def grads(b, _):
        rows = tile_at(b, BLOCK)
        low = (stack[rows, :] * jnp.concatenate([live[rows, :]] * (width // BLOCK), axis=1)).astype(BF16)
        dm[rows, :] = low
        dm_t[:, rows] = low.T
        return 0

    loop(0, ROWS // BLOCK, grads, 2)


def stage_qkv(images, width, normed, w_qkv, bias, qkv, begin, end):
    def body(c, _):
        cols = tile_at(c, TILE)
        scale = jnp.where(c < width // TILE, 1.0 / math.sqrt(HD), 1.0)
        values = (dot(normed[...], w_qkv[:, cols]) + bias[:, cols]) * scale
        for i in range(images):
            qkv[i, :, cols] = values[i * SLOT : (i + 1) * SLOT].astype(BF16)
        return 0

    loop(begin, end, body, 1)


def stage_attention(width, qkv, mask, probs, stack, i):
    low = first_lanes(SLOT)
    for p in range(H // 2):
        q2 = qkv[i, :, p * 128 : (p + 1) * 128]
        k2 = qkv[i, :, width + p * 128 : width + (p + 1) * 128]
        v2_t = qkv[i, :, 2 * width + p * 128 : 2 * width + (p + 1) * 128].T
        outs = []
        for h in range(2):
            qh = jnp.where(low if h == 0 else ~low, q2, jnp.zeros_like(q2))
            scores = dot_nt(k2, qh) + mask[i]
            exponent = jnp.exp(scores - jnp.max(scores, axis=0, keepdims=True))
            share = 1.0 / jnp.sum(exponent, axis=0, keepdims=True)
            prob = (exponent * share).astype(BF16)
            probs[2 * p + h] = prob
            outs.append(dot(v2_t[h * HD : (h + 1) * HD], prob))
        stack[pl.ds(pl.multiple_of(i * SLOT, 8), SLOT), p * 128 : (p + 1) * 128] = jnp.concatenate(outs, axis=0).T


def stage_out(width, stack, w_out, bias, token, gain, shift, att, att_t, middle, normed, normed_t):
    def low(b, _):
        rows = tile_at(b, BLOCK)
        values = stack[rows, :].astype(BF16)
        att[rows, :] = values
        att_t[:, rows] = values.T
        return 0

    loop(0, ROWS // BLOCK, low, 4)

    def body(c, _):
        cols = tile_at(c, TILE)
        middle[:, cols] = token[:, cols].astype(F32) + (dot(att[...], w_out[:, cols]) + bias[:, cols])
        return 0

    loop(0, width // TILE, body, 1)

    def norm(b, _):
        rows = tile_at(b, BLOCK)
        hat, _ = norm_parts(middle[rows, :])
        values = (hat * gain[...] + shift[...]).astype(BF16)
        normed[rows, :] = values
        normed_t[:, rows] = values.T
        return 0

    loop(0, ROWS // BLOCK, norm, 4)


def stage_mlp(width, normed, normed_t, dm, dm_t, w_up, b_up, w_down, act, dh, put_up, put_down, g_b_up, c):
    cols = tile_at(c, TILE)
    hidden = dot(normed[...], w_up[:, cols]) + b_up[:, cols]
    d_act = dot_nt(dm[...], w_down[cols, :])
    value, slope = gelu_parts(hidden)
    value = value.astype(BF16)
    grad = (d_act * slope).astype(BF16)
    act[:, cols] = value
    dh[:, cols] = grad
    g_b_up[:, cols] = jnp.sum(grad.astype(F32), axis=0, keepdims=True)
    put_up(c, dot(normed_t[...], grad).astype(BF16))
    put_down(c, dot(dm_t[...], value).astype(BF16))


def add_products(width, stack, fresh, product):
    def body(c, _):
        cols = tile_at(c, TILE)
        value = product(cols)
        stack[:, cols] = value if fresh else stack[:, cols] + value
        return 0

    loop(0, width // TILE, body, 1)


def stage_final(images, slots, width, middle, live, b_down, stack, out):
    def final(b, _):
        rows = tile_at(b, BLOCK)
        stack[rows, :] = (middle[rows, :] + (stack[rows, :] + b_down[...])) * jnp.concatenate([live[rows, :]] * (width // BLOCK), axis=1)
        return 0

    loop(0, ROWS // BLOCK, final, 2)
    for i in range(images):
        out[i] = stack[i * SLOT : i * SLOT + slots, :].astype(BF16)


def stage_middle_back(middle, gain, dm, stack, d_mid_low, g_gain, g_shift, g_b_down, g_b_out):
    for ref in (g_gain, g_shift, g_b_down, g_b_out):
        ref[...] = jnp.zeros_like(ref)

    def back(b, _):
        rows = tile_at(b, BLOCK)
        grad = stack[rows, :]
        hat, inverse = norm_parts(middle[rows, :])
        g_gain[...] += jnp.sum(grad * hat, axis=0, keepdims=True)
        g_shift[...] += jnp.sum(grad, axis=0, keepdims=True)
        own = dm[rows, :].astype(F32)
        g_b_down[...] += jnp.sum(own, axis=0, keepdims=True)
        total = own + norm_back(hat, inverse, gain[...], grad)
        middle[rows, :] = total
        low = total.astype(BF16)
        d_mid_low[rows, :] = low
        g_b_out[...] += jnp.sum(low.astype(F32), axis=0, keepdims=True)
        return 0

    loop(0, ROWS // BLOCK, back, 2)


def stage_out_back(width, att_t, d_mid_low, w_out, put_out, stack):
    def body(c, _):
        cols = tile_at(c, TILE)
        put_out(c, dot(att_t[...], d_mid_low[:, cols]).astype(BF16))
        stack[:, cols] = dot_nt(d_mid_low[...], w_out[cols, :])
        return 0

    loop(0, width // TILE, body, 1)


def stage_attention_back(width, qkv, probs, stack, i):
    low = first_lanes(SLOT)
    for p in range(H // 2):
        at_q = slice(p * 128, (p + 1) * 128)
        at_k = slice(width + p * 128, width + (p + 1) * 128)
        at_v = slice(2 * width + p * 128, 2 * width + (p + 1) * 128)
        q2, k2, v2 = qkv[i, :, at_q], qkv[i, :, at_k], qkv[i, :, at_v]
        k2_t = k2.T
        da = stack[pl.ds(pl.multiple_of(i * SLOT, 8), SLOT), at_q].astype(BF16)
        dq, dk, dv = [], 0.0, 0.0
        for h in range(2):
            pick = lambda m: jnp.where(low if h == 0 else ~low, m, jnp.zeros_like(m))
            prob = probs[2 * p + h]
            d_prob = dot_nt(pick(v2), da)
            mixed = prob.astype(F32)
            moved = mixed * d_prob
            total = jnp.sum(moved, axis=0, keepdims=True)
            ds = (moved - mixed * total).astype(BF16)
            dq.append(dot(k2_t[h * HD : (h + 1) * HD], ds))
            dk = dk + dot(ds, pick(q2))
            dv = dv + dot(prob, pick(da))
        qkv[i, :, at_q] = (jnp.concatenate(dq, axis=0).T * (1.0 / math.sqrt(HD))).astype(BF16)
        qkv[i, :, at_k] = dk.astype(BF16)
        qkv[i, :, at_v] = dv.astype(BF16)


def stage_qkv_back(images, width, d_qkv, normed_t, tile, flat, put_qkv, g_b_qkv, c):
    cols = tile_at(c, TILE)
    for i in range(images):
        tile[i * SLOT : (i + 1) * SLOT, :] = d_qkv[i, :, cols].astype(F32)
    values = tile[...]
    g_b_qkv[:, cols] = jnp.sum(values, axis=0, keepdims=True)
    low = values.astype(BF16)
    flat[:, cols] = low
    put_qkv(c, dot(normed_t[...], low).astype(BF16))


def stage_norm_back(width, flat, w_qkv, stack):
    def body(c, _):
        cols = tile_at(c, TILE)
        stack[:, cols] = dot_nt(flat[...], w_qkv[cols, :])
        return 0

    loop(0, width // TILE, body, 1)


def stage_end(images, slots, width, keep, token, gain, middle, live, stack, g_gain, g_shift, put_patches):
    for ref in (g_gain, g_shift):
        ref[...] = jnp.zeros_like(ref)

    def back(b, _):
        rows = tile_at(b, BLOCK)
        grad = stack[rows, :]
        hat, inverse = norm_parts(token[rows, :].astype(F32))
        g_gain[...] += jnp.sum(grad * hat, axis=0, keepdims=True)
        g_shift[...] += jnp.sum(grad, axis=0, keepdims=True)
        total = middle[rows, :] + norm_back(hat, inverse, gain[...], grad)
        stack[rows, :] = total * jnp.concatenate([live[rows, :]] * (width // BLOCK), axis=1)
        return 0

    loop(0, ROWS // BLOCK, back, 2)

    def scatter(i, _):
        chosen = (lax.broadcasted_iota(jnp.int32, (slots, SLOT), 0) == keep[i]).astype(F32).astype(BF16)
        values = stack[pl.ds(pl.multiple_of(i * SLOT, 8), SLOT), :]
        high = values.astype(BF16)
        rest = (values - high.astype(F32)).astype(BF16)
        put_patches(i, dot(chosen, high) + dot(chosen, rest))
        return 0

    for i in range(images):
        scatter(i, 0)


MESH = pl.DeviceIdType.MESH


class Place:
    def __init__(self):
        f, d = lax.axis_index("fsdp"), lax.axis_index("dp")
        self.z, self.x = f // 2, lax.rem(f, 2)
        self.y, self.c = d // 2, lax.rem(d, 2)
        z = self.z
        self.zs = [z, z + 1 - 2 * lax.rem(z, 2), lax.rem(z + 2, 4), 3 - z]
        self.ox, self.oy, self.oc = 1 - self.x, 1 - self.y, 1 - self.c
        self.beside = self.to(x=self.ox), self.to(y=self.oy), self.to(c=self.oc)
        self.along = [self.to(z=k) for k in self.zs]

    def to(self, z=None, x=None, y=None, c=None):
        z, x, y, c = (own if new is None else new for new, own in ((z, self.z), (x, self.x), (y, self.y), (c, self.c)))
        return (z * 2 + x, y * 2 + c)

    def sides(self):
        return self.beside


def enter(peers, meanwhile=None):
    barrier = pltpu.get_barrier_semaphore()
    for peer in peers:
        pl.semaphore_signal(barrier, inc=1, device_id=peer, device_id_type=MESH)
    if meanwhile is not None:
        meanwhile()
    pl.semaphore_wait(barrier, len(peers))


class Gather:
    def __init__(self, place, shard, full, first_cols, send, recv):
        self.place, self.shard, self.full, self.send, self.recv = place, shard, full, send, recv
        self.rows, cols = shard.shape
        self.half, self.wide, self.cut = self.rows // 2, cols // 2, first_cols
        self.started = []

    def spot(self, *args):
        return lambda: self.place_of(*args)

    def place_of(self, z, x, y, part=None, local=False):
        p = self.place
        base = 0 if local else (z * 2 + x) * self.rows
        rows = pl.ds(pl.multiple_of(base + p.c * self.half, 16), self.half)
        if y is None:
            return rows, slice(None)
        start, size = (y * self.wide, self.wide) if part is None else ((y * self.wide, self.cut) if part == 0 else (y * self.wide + self.cut, self.wide - self.cut))
        return rows, pl.ds(pl.multiple_of(start, 128), size)

    def copy(self, spot, sem, peer, local=None):
        src = self.full.at[spot] if local is None else self.shard.at[local]
        return pltpu.make_async_remote_copy(
            src_ref=src, dst_ref=self.full.at[spot], send_sem=self.send.at[sem], recv_sem=self.recv.at[sem], device_id=peer, device_id_type=MESH
        )

    def start(self, spot, sem, peer, local=None):
        def make():
            return self.copy(spot(), sem, peer, None if local is None else local())

        make().start()
        self.started.append(make)

    def arrived(self, spot, sem):
        self.copy(spot(), sem, self.place.sides()[0]).wait_recv()

    def own(self, sem):
        p = self.place
        rows = pl.ds(pl.multiple_of((p.z * 2 + p.x) * self.rows, 16), self.rows)
        return pltpu.make_async_copy(self.shard, self.full.at[rows, :], sem)

    def lines(self, *ks):
        p = self.place
        spot, local = self.spot(p.z, p.x, p.y), self.spot(p.z, p.x, p.y, None, True)
        for k in ks:
            self.start(spot, k, p.along[k], local)

    def beside(self):
        p = self.place
        side_x, side_y, _ = p.sides()
        self.start(self.spot(p.z, p.x, p.y), 4, side_x, self.spot(p.z, p.x, p.y, None, True))
        self.start(self.spot(p.z, p.x, p.oy, 1), 16, side_x, self.spot(p.z, p.x, p.oy, 1, True))

    def phase(self, name):
        if name == "own":
            self.beside()
        elif name == "zs":
            self.lines(1, 2, 3)
        elif name[0] == "z":
            self.lines(int(name[1]))
        elif name in ("spread", "cross", "share"):
            for k in range(name == "spread", 4):
                getattr(self, name)(k)
        else:
            (self.spread if name[0] == "s" else self.cross)(int(name[1]))

    def spread(self, k):
        p = self.place
        side_x, side_y, _ = p.sides()
        spot = self.spot(p.zs[k], p.x, p.y)
        self.arrived(spot, k)
        self.start(spot, 4 + k, side_x)
        self.start(spot, 8 + k, side_y)

    def cross(self, k):
        p = self.place
        side_x, side_y, _ = p.sides()
        self.arrived(self.spot(p.zs[k], p.ox, p.y), 4 + k)
        self.start(self.spot(p.zs[k], p.ox, p.y, 0), 12 + k, side_y)
        if k:
            self.arrived(self.spot(p.zs[k], p.x, p.oy), 8 + k)
            self.start(self.spot(p.zs[k], p.x, p.oy, 1), 16 + k, side_x)

    def share(self, k):
        p = self.place
        core = p.sides()[2]
        if k:
            self.start(self.spot(p.zs[k], p.x, None), 20 + k, core)
        self.arrived(self.spot(p.zs[k], p.ox, p.oy, 0), 12 + k)
        self.arrived(self.spot(p.zs[k], p.ox, p.oy, 1), 16 + k)
        self.start(self.spot(p.zs[k], p.ox, None), 24 + k, core)

    def finish(self):
        p = self.place

        def other(z, x):
            return lambda: (pl.ds(pl.multiple_of((z * 2 + x) * self.rows + (p.oc) * self.half, 16), self.half), slice(None))

        for k in range(4):
            if k:
                self.arrived(other(p.zs[k], p.x), 20 + k)
            self.arrived(other(p.zs[k], p.ox), 24 + k)

    def drain(self):
        for make in self.started:
            make().wait_send()


class Reduce:
    def __init__(self, place, source, held, core, diag_x, diag_y, side_x, side_y, line, final, send, recv):
        self.place, self.source, self.held, self.core = place, source, held, core
        self.diag_x, self.diag_y, self.side_x, self.side_y, self.line, self.final = diag_x, diag_y, side_x, side_y, line, final
        self.send, self.recv, self.started = send, recv, []
        self.own4 = self.own = None
        if diag_y is not None:
            self.rows, self.wide = side_x.shape[1:]
            self.by_rows = diag_y.shape[2] == self.wide
            self.cut = diag_y.shape[1] if self.by_rows else diag_y.shape[2]

    def part(self, second):
        bounds = pl.ds(self.cut, (self.rows if self.by_rows else self.wide) - self.cut) if second else pl.ds(0, self.cut)
        return (bounds, slice(None)) if self.by_rows else (slice(None), bounds)

    def hold(self, z, x, y, *rest):
        if self.held is None:
            return (z, x, self.place.c, y) + rest
        return (z, x, y) + rest

    @property
    def home(self):
        return self.source if self.held is None else self.held

    def copy(self, src, dst, sem, peer):
        return pltpu.make_async_remote_copy(src_ref=src, dst_ref=dst, send_sem=self.send.at[sem], recv_sem=self.recv.at[sem], device_id=peer, device_id_type=MESH)

    def start(self, src, dst, sem, peer):
        def make():
            return self.copy(src(), dst() if callable(dst) else dst, sem, peer)

        make().start()
        self.started.append(make)

    def arrived(self, dst, sem):
        self.copy(dst, dst, sem, self.place.sides()[0]).wait_recv()

    def begin(self, own=None):
        p = self.place
        self.start(lambda: self.source.at[:, :, p.oc], self.core, 0, p.sides()[2])
        self.own = own
        if own is not None:
            own.start()

    def add_core(self, x, y):
        def body(z, _):
            spot = self.hold(z, x, y)
            self.home[spot] = self.home[spot] + self.core[z, x, y]
            return 0

        lax.fori_loop(0, 4, body, 0)

    def add(self, x, y, part, buffer):
        def body(z, _):
            spot = self.hold(z, x, y, *part)
            self.home[spot] = self.home[spot] + buffer[z]
            return 0

        lax.fori_loop(0, 4, body, 0)

    def step_core(self):
        p = self.place
        side_x, side_y, _ = p.sides()
        if self.own is not None:
            self.own.wait()
        self.arrived(self.core, 0)
        for x, y in ((p.ox, p.oy), (p.ox, p.y), (p.x, p.oy), (p.x, p.y)):
            self.add_core(x, y)

    def step_open(self):
        p = self.place
        side_x, side_y, _ = p.sides()
        every = slice(None)
        self.start(lambda: self.home.at[self.hold(every, p.ox, p.oy, *self.part(True))], self.diag_x, 1, side_x)
        self.start(lambda: self.home.at[self.hold(every, p.ox, p.oy, *self.part(False))], self.diag_y, 2, side_y)

    def step_diag(self):
        p = self.place
        side_x, side_y, _ = p.sides()
        every = slice(None)
        self.arrived(self.diag_y, 2)
        self.add(p.ox, p.y, self.part(False), self.diag_y)
        self.start(lambda: self.home.at[self.hold(every, p.ox, p.y)], self.side_x, 3, side_x)
        self.arrived(self.diag_x, 1)
        self.add(p.x, p.oy, self.part(True), self.diag_x)
        self.start(lambda: self.home.at[self.hold(every, p.x, p.oy)], self.side_y, 4, side_y)

    def step_sum(self):
        p = self.place
        whole = (slice(None), slice(None))
        self.arrived(self.side_x, 3)
        self.add(p.x, p.y, whole, self.side_x)
        self.arrived(self.side_y, 4)
        self.add(p.x, p.y, whole, self.side_y)

    def mine(self, z):
        if self.own4 is not None:
            return self.own4.at[z]
        return self.home.at[self.hold(z, self.place.x, self.place.y)]

    def step_send(self):
        p = self.place
        for k in (1, 2, 3):
            self.start(lambda k=k: self.mine(p.zs[k]), lambda k=k: self.line.at[k - 1], 4 + k, p.along[k])

    def step_side(self):
        self.step_sum()
        self.step_send()

    def step_line(self):
        p = self.place
        total = self.mine(p.z)[...].astype(F32)
        for k in (1, 2, 3):
            self.arrived(self.line.at[k - 1], 4 + k)
            total = total + self.line[k - 1].astype(F32)
        self.final[p.c, p.y] = total.astype(BF16)
        self.start(lambda: self.final.at[p.c, p.y], lambda: self.final.at[p.c, p.y], 8, p.sides()[1])

    def step_share(self):
        p = self.place
        self.arrived(self.final.at[p.c, p.oy], 8)
        self.start(lambda: self.final.at[p.c], lambda: self.final.at[p.c], 9, p.sides()[2])

    def finish(self):
        self.arrived(self.final.at[self.place.oc], 9)

    def drain(self):
        for make in self.started:
            make().wait_send()


class SmallReduce:
    def __init__(self, place, home, core, side_y, side_x, line, send, recv):
        self.place, self.home, self.core, self.side_y, self.side_x, self.line = place, home, core, side_y, side_x, line
        self.send, self.recv, self.started = send, recv, []

    copy, start, arrived, drain = Reduce.copy, Reduce.start, Reduce.arrived, Reduce.drain

    def begin(self):
        self.start(lambda: self.home, self.core, 0, self.place.sides()[2])

    def step_core(self, sent):
        p = self.place
        self.arrived(self.core, 0)
        sent[...] = self.home[...] + self.core[...]
        self.start(lambda: sent, self.side_y, 1, p.sides()[1])

    def step_y(self, sent, total):
        p = self.place
        self.arrived(self.side_y, 1)
        total[...] = sent[...] + self.side_y[...]
        self.start(lambda: total.at[:, p.ox], self.side_x, 2, p.sides()[0])

    def step_x(self, total):
        p = self.place
        self.arrived(self.side_x, 2)
        for z in range(4):
            self.side_x[z] = self.side_x[z] + total[z, p.x]
        for k in (1, 2, 3):
            self.start(lambda k=k: self.side_x.at[p.zs[k]], lambda k=k: self.line.at[k - 1], 2 + k, p.along[k])

    def step_line(self, out):
        total = self.side_x[self.place.z]
        for k in (1, 2, 3):
            self.arrived(self.line.at[k - 1], 2 + k)
            total = total + self.line[k - 1]
        out[...] = total


GATHER_PLAN = (
    (("k", "own"), ("v", "own"), ("o", "own"), ("p0", "own"), ("q", "z1"), ("k", "z1"), ("q", "z2"), ("k", "z2"), ("k", "z3"), ("q", "s1"), ("k", "s1"),),
    (("v", "z1"), ("q", "z3"), ("k", "c0"), ("k", "s3"),),
    (("v", "z2"), ("v", "z3"),),
    (),
    (("v", "s1"), ("q", "s2"), ("q", "c1"),),
    (("o", "zs"), ("k", "s2"), ("q", "s3"),),
    (("q", "own"), ("p0", "zs"), ("v", "c0"), ("v", "s2"), ("v", "s3"), ("k", "c2"), ("q", "c3"), ("k", "c3"),),
    (("q", "c0"), ("v", "c1"), ("q", "c2"), ("v", "c2"), ("v", "c3"),),
    (("k", "c1"), ("o", "spread"), ("q", "share"), ("k", "share"),),
    (("p1", "own"), ("p1", "zs"), ("o", "cross"), ("v", "share"),),
    (("p0", "spread"),),
    (),
    (),
    (("p2", "zs"), ("p1", "spread"), ("p0", "cross"), ("o", "share"),),
    (),
    (("p2", "own"),),
    (("p1", "cross"), ("p0", "share"),),
    (("p2", "spread"),),
    (),
    (),
    (("p1", "share"),),
    (("p2", "cross"),),
    (),
    (),
    (("p2", "share"),),
    (),
    (),
    (),
    (),
    (),
)
MERGE_PLAN = (22, 25, 26)
REDUCE_PLAN = (
    ("m0", (5, 21)),
    ("m1", (0, 4, 9, 14, 22)),
    ("m2", (2, 8, 13, 19, 21)),
    ("o", (7, 12, 15, 20, 21)),
    ("q", (13, 15, 17, 19, 21)),
    ("k", (14, 16, 19, 21, 21)),
    ("v", (14, 18, 19, 21, 22)),
)


VMEM = pl.BlockSpec(memory_space=pltpu.VMEM)
ANY = pl.BlockSpec(memory_space=pl.ANY)
LIMIT = 61 * 1024 * 1024
THIRD = 1024


def call(body, outs, scratch, args, name):
    return pl.pallas_call(
        body,
        out_shape=[jax.ShapeDtypeStruct(*o) for o in outs],
        in_specs=[VMEM] * len(args),
        out_specs=[VMEM] * len(outs),
        scratch_shapes=[pltpu.VMEM(*s) for s in scratch],
        compiler_params=pltpu.CompilerParams(vmem_limit_bytes=LIMIT),
        name=name,
    )(*args)


class Later:
    def __init__(self, sems):
        self.sems, self.flights = sems, {}

    def start(self, name, src, dst):
        self.plan(name, src, dst)
        self.flights[name]().start()

    def plan(self, name, src, dst):
        sem = len(self.flights)

        def make():
            return pltpu.make_async_copy(*(r() if callable(r) else r for r in (src, dst)), self.sems.at[sem])

        self.flights[name] = make

    def wait(self, *names):
        for name in names:
            self.flights[name]().wait()


def first_plain(
    images, slots, width, patches, keep, cot, vectors, w_qkv, w_out,
    token, n1t, dm, dmt, live, qkv, probs, att_t, middle, n2, n2t, stack, normed, mask, att, bias,
):
    bias[...] = jnp.concatenate([vectors[2:3, :], jnp.zeros((1, width), F32), vectors[3:4, :]], axis=1)
    stage_gather(images, slots, patches, keep, stack, live, mask, token)
    stage_norm(vectors[0:1, :], vectors[1:2, :], token, normed, n1t)
    stage_grads(images, slots, width, cot, stack, live, dm, dmt)
    stage_qkv(images, width, normed, w_qkv, bias, qkv, 0, 3 * width // TILE)
    for i in range(images):
        stage_attention(width, qkv, mask, probs.at[pl.ds(i * H, H)], stack, i)
    stage_out(width, stack, w_out, vectors.at[4:5, :], token, vectors.at[5:6, :], vectors.at[6:7, :], att, att_t, middle, n2, n2t)


def first_kernel(
    images, slots, width,
    patches, keep, cot, vec, s_qkv, s_out, s_up, s_down,
    vectors, g_b_up, h_token, h_n1t, h_dm, h_live, h_qkv, h_probs, h_att_t, h_middle, h_wqkv, h_wout, h_up, h_down, h_act, h_dh, h_gup, h_gdown, h_up1, h_down1, h_own_up, h_own_down,
    stack, normed, mask, token, n1t, dm, dmt, live, qkv, probs, att_t, middle, f_qkv, f_out, f_up, f_down, s_up3, act_, dh, g_up, g_down, up_core, down_core, up_dx, up_dy, up_sx, up_sy, dn_dx, dn_dy, dn_sx, dn_sy,
    vecs, bias, b_up, q_send, q_recv, m_send, m_recv, v_send, v_recv, own, saves, probs_sem, r_send, r_recv, w_send, w_recv,
):
    place = Place()
    _, side_y, side_c = place.sides()
    flat = [place.to(z=place.zs[k], x=x) for k in range(4) for x in (place.x, place.ox)][1:]
    later = Later(saves)

    def before():
        for t in range(3):
            for f in range(8):
                s_up3[t, :, f * 128 : f * 128 + 128] = s_up[:, f * 384 + t * 128 : f * 384 + t * 128 + 128]
        stage_gather(images, slots, patches, keep, stack, live, mask, token)
        later.start("live", live, h_live)
        later.start("token", token, h_token)
        stage_grads(images, slots, width, cot, stack, live, dm, dmt)
        later.start("dm", dm, h_dm)

    enter(flat + [side_y, side_c], before)
    columns = [slice(m * width, (m + 1) * width) for m in range(3)]
    g_qkv = [Gather(place, s_qkv.at[:, columns[m]], f_qkv.at[:, columns[m]], 128 if m == 2 else 256, q_send.at[m], q_recv.at[m]) for m in range(3)]
    g_out = Gather(place, s_out, f_out, 256, q_send.at[3], q_recv.at[3])
    g_ups = [Gather(place, s_up3.at[t], f_up.at[t], (256, 384, 256)[t], m_send.at[t], m_recv.at[t]) for t in range(3)]
    g_downs = [Gather(place, s_down.at[t * 128 : t * 128 + 128], f_down.at[t], 256, m_send.at[3 + t], m_recv.at[3 + t]) for t in range(3)]
    groups = {"q": g_qkv[:1], "k": g_qkv[1:2], "v": g_qkv[2:], "o": [g_out]}
    groups.update({f"p{t}": [g_ups[t], g_downs[t]] for t in range(3)})
    every = g_qkv + [g_out] + [g for t in range(3) for g in (g_ups[t], g_downs[t])]
    mine = place.z * 2 + place.x
    tiny = []
    for j, peer in enumerate(flat):
        copy = pltpu.make_async_remote_copy(src_ref=vec, dst_ref=vecs.at[mine], send_sem=v_send.at[j], recv_sem=v_recv.at[j], device_id=peer, device_id_type=MESH)
        copy.start()
        tiny.append(copy)
    vecs[mine] = vec[...]
    core = place.sides()[2]
    swaps = {
        (name, t): pltpu.make_async_remote_copy(
            src_ref=g.at[t, :, :, place.oc], dst_ref=buffer.at[t], send_sem=r_send.at[2 * t + j], recv_sem=r_recv.at[2 * t + j], device_id=core, device_id_type=MESH
        )
        for t in range(2)
        for j, (name, g, buffer) in enumerate((("up", g_up, up_core), ("down", g_down, down_core)))
    }
    early = (
        Reduce(place, None, up_core.at[0], None, up_dx, up_dy, up_sx, up_sy, None, None, w_send.at[0], w_recv.at[0]),
        Reduce(place, None, down_core.at[0], None, dn_dx, dn_dy, dn_sx, dn_sy, None, None, w_send.at[1], w_recv.at[1]),
    )

    def merge(t):
        for name, g, buffer in (("up", g_up, up_core), ("down", g_down, down_core)):
            swaps[name, t].wait_recv()

            def body(z, _, g=g, buffer=buffer):
                buffer[t, z] = buffer[t, z] + g[t, z, :, place.c]
                return 0

            lax.fori_loop(0, 4, body, 0)
        if t == 0:
            for r in early:
                r.step_open()
        else:
            later.start("up_sum1", lambda: up_core.at[1], h_up1)
            later.start("down_sum1", lambda: down_core.at[1], h_down1)

    def act(slot):
        for group, phase in GATHER_PLAN[slot]:
            for g in groups[group]:
                g.phase(phase)
        if slot == MERGE_PLAN[0]:
            merge(0)
        if slot == MERGE_PLAN[1]:
            for r in early:
                r.step_diag()
        if slot == MERGE_PLAN[2]:
            merge(1)

    act(0)
    locals_ = [g.own(own.at[j]) for j, g in enumerate(every)]
    for copy in locals_:
        copy.start()
    for slot in range(1, 5):
        act(slot)
    for copy in tiny:
        copy.wait_recv()
    vectors[...] = jnp.concatenate([vecs[f][:, :96] for f in range(8)], axis=1).astype(F32)
    act(5)
    stage_norm(vectors[0:1, :], vectors[1:2, :], token, normed, n1t)
    later.start("n1t", n1t, h_n1t)
    for f in range(8):
        row = jnp.concatenate([vecs[f][8 + j : 9 + j, :96] for j in range(4)], axis=1).astype(F32)
        for t in range(3):
            b_up[t, :, f * 128 : f * 128 + 128] = row[:, t * 128 : t * 128 + 128]
    bias[...] = jnp.concatenate([vectors[2:3, :], jnp.zeros((1, width), F32), vectors[3:4, :]], axis=1)
    act(6)
    act(7)
    for m in range(3):
        act(8 + m)
        locals_[m].wait()
        g_qkv[m].finish()
        stage_qkv(images, width, normed, f_qkv, bias, qkv, m * width // TILE, (m + 1) * width // TILE)
    later.start("w_qkv", f_qkv, h_wqkv)
    later.start("qkv", qkv, h_qkv)

    def save_probs(slot, i):
        return pltpu.make_async_copy(probs.at[slot], h_probs.at[pl.ds(i * H, H)], probs_sem.at[slot])

    def attend(i, _):
        slot = lax.rem(i, 2)
        for j in range(5):
            pl.when(i == j)(lambda j=j: act(11 + j))
        pl.when(i >= 2)(lambda: save_probs(slot, i - 2).wait())
        stage_attention(width, qkv, mask, probs.at[slot], stack, i)
        save_probs(slot, i).start()
        return 0

    lax.fori_loop(0, images, attend, 0)
    for i in range(images - 2, images):
        save_probs(i % 2, i).wait()
    act(16)
    locals_[3].wait()
    g_out.finish()
    later.start("w_out", f_out, h_wout)
    later.wait("n1t")
    n2t = n1t
    stage_out(width, stack, f_out, vectors.at[4:5, :], token, vectors.at[5:6, :], vectors.at[6:7, :], normed, att_t, middle, normed, n2t)
    later.start("att_t", att_t, h_att_t)
    later.start("middle", middle, h_middle)
    for t in range(3):
        for part in range(2):
            for name, src, dst in (("act", act_, h_act), ("dh", dh, h_dh)):
                cols = slice(part * 512, part * 512 + 512)
                later.plan(f"{name}{t}{part}", lambda src=src, cols=cols: src.at[:, cols], lambda dst=dst, t=t, cols=cols: dst.at[t, :, cols])

    def enter_third(t):
        locals_[4 + 2 * t].wait()
        locals_[5 + 2 * t].wait()
        g_ups[t].finish()
        g_downs[t].finish()
        later.start(f"up{t}", lambda: f_up.at[t], lambda: h_up.at[t])
        later.start(f"down{t}", lambda: f_down.at[t], lambda: h_down.at[t])
        if t:
            later.wait(f"act{t - 1}0", f"dh{t - 1}0")
        if t == 2:
            for name in ("up", "down"):
                swaps[name, 0].wait_send()

    def middle_third(t):
        if t:
            later.wait(f"act{t - 1}1", f"dh{t - 1}1")

    def save_part(t, part):
        later.flights[f"act{t}{part}"]().start()
        later.flights[f"dh{t}{part}"]().start()
        if part and t < 2:
            swaps["up", t].start()
            swaps["down", t].start()
        elif part:
            later.start("g_up2", lambda: g_up.at[0], h_gup)
            later.start("g_down2", lambda: g_down.at[0], h_gdown)

    def feed(step, _):
        t, c = step // 4, step % 4
        slot = t % 2
        for j in range(12):
            if GATHER_PLAN[17 + j] or 17 + j in MERGE_PLAN:
                pl.when(step == j)(lambda j=j: act(17 + j))
        for j in range(3):
            pl.when(step == 4 * j)(lambda j=j: enter_third(j))
            pl.when(step == 4 * j + 2)(lambda j=j: middle_third(j))

        def put_up(c, value):
            y, at = c // 2, tile_at(c % 2, TILE)
            g_up[slot, :, :, :, y, :, at] = value.reshape(4, 2, 2, 48, TILE)

        def put_down(c, value):
            for x in range(2):
                g_down[slot, c, x] = value[:, x * 128 : (x + 1) * 128].reshape(2, 2, 192, 128)

        stage_mlp(width, normed, n2t, dm, dmt, f_up.at[t], b_up.at[t], f_down.at[t], act_, dh, put_up, put_down, g_b_up.at[t], c)
        for j in range(3):
            for part in range(2):
                pl.when(step == 4 * j + 2 * part + 1)(lambda j=j, part=part: save_part(j, part))
        return 0

    lax.fori_loop(0, 12, feed, 0)
    act(29)
    for r, h, buffer in ((early[0], h_own_up, up_core), (early[1], h_own_down, down_core)):
        r.step_sum()
        later.start(f"own{h is h_own_up}", buffer.at[0, :, place.x, place.y], h)
    waited = {"n1t"} | {f"{n}{t}{p}" for n in ("act", "dh") for t in range(2) for p in range(2)}
    for name in ("up", "down"):
        swaps[name, 1].wait_send()
    later.wait(*(n for n in later.flights if n not in waited))
    for copy in tiny:
        copy.wait_send()
    for g in every + list(early):
        g.drain()


def second_plain(
    images, slots, width, hidden_width,
    n2, n2t, dm, dmt, w_up, b_up, w_down, b_d, middle_in, live, gain2,
    out, middle, d_low, g_up, g_down, g_b_up, g_g2, g_s2, g_bd, g_bo, act, dh, stack,
):
    middle[...] = middle_in[...]

    def put(ref, c, value):
        ref[:, tile_at(c, TILE)] = value

    feed = functools.partial(stage_mlp, width, n2, n2t, dm, dmt, w_up, b_up, w_down, act, dh, functools.partial(put, g_up), functools.partial(put, g_down), g_b_up)
    loop(0, hidden_width // TILE, lambda c, _: feed(c), 1)
    add_products(width, stack, True, lambda cols: dot(act[...], w_down[:, cols]))
    stage_final(images, slots, width, middle, live, b_d, stack, out)
    add_products(width, stack, True, lambda cols: dot_nt(dh[...], w_up[cols, :]))
    stage_middle_back(middle, gain2, dm, stack, d_low, g_g2, g_s2, g_bd, g_bo)


def third_plain(
    images, slots, width, d_low, att_t, w_out, qkv_in, probs, n1t, w_qkv, token, gain, mid, live, keep,
    g_out, g_qkv, g_b, g_g1, g_s1, gp, stack, tile, flat, qkv,
):
    def put(ref, c, value):
        ref[:, tile_at(c, TILE)] = value

    def put_patches(i, value):
        gp[i] = value

    qkv[...] = qkv_in[...]
    tile[...] = jnp.zeros_like(tile)
    stage_out_back(width, att_t, d_low, w_out, functools.partial(put, g_out), stack)
    for i in range(images):
        stage_attention_back(width, qkv, probs.at[pl.ds(i * H, H)], stack, i)
    back = functools.partial(stage_qkv_back, images, width, qkv, n1t, tile, flat, functools.partial(put, g_qkv), g_b)
    loop(0, 3 * width // TILE, lambda c, _: back(c), 1)
    stage_norm_back(width, flat, w_qkv, stack)
    stage_end(images, slots, width, keep, token, gain, mid, live, stack, g_g1, g_s1, put_patches)


def second_kernel(
    images, slots, width,
    keep, vectors, s_bup, h_token, h_n1t, h_dm, h_live, h_qkv, h_probs, h_att_t, h_middle, h_wqkv, h_wout, h_up, h_down, h_act, h_dh, h_gup, h_gdown, h_up1, h_down1, h_own_up, h_own_down,
    gp, out_tokens, o_qkv, o_out, o_up, o_down, e_small,
    e_up, e_down, e_out, e_q, e_k, e_v,
    stack, tile, flat, qkv, probs, t_a, t_b, r_a, r_b, mid, live, w_qkv, w_out, stage, g_b, g_g1, g_s1, g_g2, g_s2, g_bd, g_bo, g_attn,
    up_held, up_own, up_core, up_dx, up_dy, up_sx, up_sy, up_ln, dn_held, dn_own, dn_core, dn_dx, dn_dy, dn_sx, dn_sy, dn_ln,
    core4, dx4, dy4, sx4, sy4, ln4, v_home, v_core, v_sy, v_sx, v_ln, v_sent, v_total,
    send, recv, v_send, v_recv, own, loads, probs_sem, out_sem,
):
    place = Place()
    enter(place.along[1:] + list(place.sides()))
    def reduce_third(t, source, held, own4, core, dx, dy, sx, sy, ln, e, sem):
        sems = send.at[sem + t], recv.at[sem + t]
        if t == 0:
            r = Reduce(place, None, None, None, None, None, None, None, ln.at[0], e.at[0], *sems)
            r.own4 = own4
            return r
        return Reduce(place, source, held.at[t - 1], core, dx.at[t - 1], dy.at[t - 1], sx.at[t - 1], sy.at[t - 1], ln.at[t], e.at[t], *sems)

    r_up = [reduce_third(t, h_gup, up_held, up_own, up_core, up_dx, up_dy, up_sx, up_sy, up_ln, e_up, 0) for t in range(3)]
    r_down = [reduce_third(t, h_gdown, dn_held, dn_own, dn_core, dn_dx, dn_dy, dn_sx, dn_sy, dn_ln, e_down, 3) for t in range(3)]
    mlp = [(r_up[t], r_down[t]) for t in range(3)]
    r_q, r_k, r_v, r_out = (
        Reduce(place, g_attn.at[m], None, core4.at[m], dx4.at[m], dy4.at[m], sx4.at[m], sy4.at[m], ln4.at[m], e, send.at[6 + m], recv.at[6 + m])
        for m, e in enumerate((e_q, e_k, e_v, e_out))
    )
    small = SmallReduce(place, v_home, v_core, v_sy, v_sx, v_ln, v_send, v_recv)
    later = Later(loads)
    slots_ = [flat.at[:, 0:THIRD], flat.at[:, THIRD : 2 * THIRD]]
    groups = {"m0": mlp[0], "m1": mlp[1], "m2": mlp[2], "o": (r_out,), "q": (r_q,), "k": (r_k,), "v": (r_v,)}

    def act(slot):
        for phase in ("open", "core", "diag", "side", "line", "share"):
            for group, slots_of in REDUCE_PLAN:
                phases = {2: ("line", "share"), 5: ("open" if group == "m1" else "core", "diag", "side", "line", "share")}[len(slots_of)]
                if (phase, slot) in zip(phases, slots_of):
                    for r in groups[group]:
                        getattr(r, "step_" + phase)()
                        if phase == "core":
                            r.step_open()

    early = [
        pltpu.make_async_copy(h, into, own.at[j])
        for j, (h, into) in enumerate(((h_own_up, up_own), (h_own_down, dn_own), (h_up1, up_held.at[0]), (h_down1, dn_held.at[0])))
    ]
    for copy in early:
        copy.start()
    later.start("dh0", h_dh.at[0], slots_[0])
    later.start("up0", h_up.at[0], t_a)
    for j, (r, h, into) in enumerate(((r_up[2], h_gup, up_held), (r_down[2], h_gdown, dn_held))):
        r.begin(pltpu.make_async_copy(h.at[:, :, place.c], into.at[1], own.at[4 + j]))
    later.start("dh1", h_dh.at[1], slots_[1])
    later.start("up1", h_up.at[1], t_b)
    for copy, r in zip(early[:2], mlp[0]):
        copy.wait()
        r.step_send()
    for copy in early[2:]:
        copy.wait()
    act(0)
    for name, src, dst in (("mid", h_middle, mid), ("dm", h_dm, r_a), ("live", h_live, live), ("w_out", h_wout, w_out), ("qkv", h_qkv, qkv), ("w_qkv", h_wqkv, w_qkv)):
        later.start(name, src, dst)

    def load_probs(i):
        slot = i % 2
        return pltpu.make_async_copy(h_probs.at[pl.ds(i * H, H)], probs.at[slot], probs_sem.at[slot])

    load_probs(0).start()
    later.wait("dh0", "up0")
    act(1)
    add_products(width, stack, True, lambda cols: dot_nt(slots_[0][...], t_a[cols, :]))
    later.start("dh2", h_dh.at[2], slots_[0])
    later.start("up2", h_up.at[2], t_a)
    act(2)
    later.wait("dh1", "up1")
    add_products(width, stack, False, lambda cols: dot_nt(slots_[1][...], t_b[cols, :]))
    later.start("att_t", h_att_t, t_b)
    act(3)
    later.wait("dh2", "up2")
    add_products(width, stack, False, lambda cols: dot_nt(slots_[0][...], t_a[cols, :]))
    later.start("n1t", h_n1t, t_a)
    act(4)
    later.wait("mid", "dm")
    gain2 = vectors.at[5:6, :]
    stage_middle_back(mid, gain2, r_a, stack, r_b, g_g2, g_s2, g_bd, g_bo)
    later.start("token", h_token, r_a)

    def put(m, c, value):
        for j in range(2):
            col = 2 * c + j
            y, off = (col % 6) // 3, col % 3
            at = tile_at(off, 128)
            g_attn[col // 6 if m is None else m, :, :, :, y, :, at] = value[:, j * 128 : (j + 1) * 128].reshape(4, 2, 2, 48, 128)

    act(5)
    later.wait("att_t", "w_out", "qkv")
    stage_out_back(width, t_b, r_b, w_out, functools.partial(put, 3), stack)
    r_out.begin()

    def back(i, _):
        for j in range(5):
            pl.when(i == j)(lambda j=j: act(6 + j))
        load_probs(i).wait()
        pl.when(i + 1 < images)(lambda: load_probs(i + 1).start())
        stage_attention_back(width, qkv, probs.at[lax.rem(i, 2)], stack, i)
        return 0

    lax.fori_loop(0, images, back, 0)
    later.wait("n1t")
    tile[...] = jnp.zeros_like(tile)
    project = functools.partial(stage_qkv_back, images, width, qkv, t_a, tile, flat, functools.partial(put, None), g_b)
    third = width // TILE

    def project_tile(c, _):
        for m in range(3):
            pl.when(c == m * third)(lambda m=m: act(11 + m))
        project(c)
        for m, r in enumerate((r_q, r_k, r_v)):
            pl.when(c == m * third + third - 1)(lambda r=r: r.begin())
        return 0

    lax.fori_loop(0, 3 * third, project_tile, 0)
    act(14)
    later.wait("w_qkv")
    stage_norm_back(width, flat, w_qkv, stack)
    later.start("act0", h_act.at[0], slots_[0])
    later.start("act1", h_act.at[1], slots_[1])
    later.start("down0", h_down.at[0], r_b)
    act(15)
    later.wait("token", "live")
    flights = []

    def put_patches(i, value):
        if i >= 2:
            flights[i - 2].wait()
        stage[i % 2] = value
        copy = pltpu.make_async_copy(stage.at[i % 2], gp.at[i], out_sem.at[i % 2])
        copy.start()
        flights.append(copy)

    stage_end(images, slots, width, keep, r_a, vectors.at[0:1, :], mid, live, stack, g_g1, g_s1, put_patches)
    later.start("middle", h_middle, mid)
    later.start("down1", h_down.at[1], r_a)
    act(16)
    v_home[...] = jnp.zeros_like(v_home)
    for j, (ref, base) in enumerate(((g_g1, 0), (g_s1, 0), (g_b, 0), (g_b, 2 * width), (g_bo, 0), (g_g2, 0), (g_s2, 0), (g_bd, 0))):
        row = ref[:, base : base + width]
        for f in range(8):
            v_home[f // 2, f % 2, j : j + 1, :96] = row[:, 96 * f : 96 * f + 96]
    for f in range(8):
        row = jnp.concatenate([s_bup[t, :, f * 128 : f * 128 + 128] for t in range(3)], axis=1)
        for j in range(4):
            v_home[f // 2, f % 2, 8 + j : 9 + j, :96] = row[:, 96 * j : 96 * j + 96]
    small.begin()
    act(17)
    later.wait("act0", "down0")
    add_products(width, stack, True, lambda cols: dot(slots_[0][...], r_b[:, cols]))
    later.start("act2", h_act.at[2], slots_[0])
    later.start("down2", h_down.at[2], r_b)
    small.step_core(v_sent)
    act(18)
    later.wait("act1", "down1")
    add_products(width, stack, False, lambda cols: dot(slots_[1][...], r_a[:, cols]))
    small.step_y(v_sent, v_total)
    act(19)
    later.wait("act2", "down2", "middle")
    add_products(width, stack, False, lambda cols: dot(slots_[0][...], r_b[:, cols]))
    small.step_x(v_total)
    act(20)
    stage_final(images, slots, width, mid, live, vectors.at[7:8, :], stack, out_tokens)
    small.step_line(e_small)
    act(21)
    act(22)
    for r in r_up + r_down:
        r.finish()
    for t in range(3):
        for c in range(2):
            for y in range(2):
                for f in range(4):
                    col = (4 * y + f) * 384 + t * 128
                    o_up[48 * c : 48 * c + 48, col : col + 128] = e_up[t, c, y, :, f * 128 : f * 128 + 128]
        o_down[t * 128 : t * 128 + 128, :] = e_down[t].reshape(width, 128).T
    half = width // 2

    def place_blocks(ref, base, e):
        for c in range(2):
            for y in range(2):
                ref[48 * c : 48 * c + 48, base + y * half : base + y * half + half] = e[c, y]

    r_out.finish()
    place_blocks(o_out, 0, e_out)
    for m, (r, e) in enumerate(((r_q, e_q), (r_k, e_k), (r_v, e_v))):
        r.finish()
        place_blocks(o_qkv, m * width, e)
    for copy in flights[-2:]:
        copy.wait()
    for r in r_up + r_down + [r_out, r_q, r_k, r_v, small]:
        r.drain()


def shards(
    linked,
    patches, keep, ln1_gain, ln1_bias, w_qkv, b_query, b_value, w_out, b_out,
    ln2_gain, ln2_bias, w_up, b_up, w_down, b_down, cotangent,
):
    images, slots = keep.shape
    width = patches.shape[2]
    hidden_width = w_up.shape[1]
    keep_pad = jnp.pad(keep, ((0, 0), (0, SLOT - slots)), constant_values=-1).reshape(images, 1, SLOT)
    part = ln1_gain.shape[0]
    singles = [v.reshape(1, part) for v in (ln1_gain, ln1_bias, b_query, b_value, b_out, ln2_gain, ln2_bias, b_down)]
    rows_low, rows_wide = ((ROWS, width), BF16), ((ROWS, width), F32)
    cols_low = ((width, ROWS), BF16)
    live_like, mask_like = ((ROWS, BLOCK), F32), ((images, SLOT, SLOT), F32)
    heads_like = ((images, SLOT, 3 * width), BF16)
    probs_like = ((images * H, SLOT, SLOT), BF16)
    row_like = ((1, width), F32)

    if linked:
        half = width // 2
        vec = jnp.concatenate(singles + [b_up.reshape(4, part)], axis=0)
        vec = jnp.pad(vec, ((0, 4), (0, BLOCK - part)))
        full = lambda v: ((v.shape[0] * 8, v.shape[1]), BF16)
        up3, down3, hid3 = ((3, width, THIRD), BF16), ((3, THIRD, width), BF16), ((3, ROWS, THIRD), BF16)
        gup_like, gdown_like = (4, 2, 2, 2, 48, THIRD // 2), (4, 2, 2, 2, width // 4, 128)
        outs = [
            ((16, width), F32), ((3, 1, THIRD), F32), rows_low, cols_low, rows_low, live_like, heads_like, probs_like, cols_low, rows_wide,
            full(w_qkv), full(w_out), up3, down3, hid3, hid3, (gup_like, BF16), (gdown_like, BF16), ((4, 2) + gup_like[3:], BF16), ((4, 2) + gdown_like[3:], BF16),
            ((4,) + gup_like[4:], BF16), ((4,) + gdown_like[4:], BF16),
        ]
        scratch = [
            rows_wide, rows_low, mask_like, rows_low, cols_low, rows_low, cols_low, live_like, heads_like, ((2, H, SLOT, SLOT), BF16), cols_low,
            rows_wide, full(w_qkv), full(w_out), up3, down3, ((3, part, THIRD), BF16), hid3[0][1:], hid3[0][1:], (2,) + gup_like, (2,) + gdown_like,
            (2, 4, 2) + gup_like[3:], (2, 4, 2) + gdown_like[3:],
        ]
        for r, w, first, other in ((48, THIRD // 2, (4, 48, 128), (4, 48, THIRD // 2 - 128)), (width // 4, 128, (4, 64, 128), (4, width // 4 - 64, 128))):
            scratch += [other, first, (4, r, w), (4, r, w)]
        scratch += [((8, 16, BLOCK), BF16), ((1, 3 * width), F32), ((3, 1, THIRD), F32)]
        scratch = [s if isinstance(s[0], tuple) else (s, BF16) for s in scratch]
        vectors, g_b_up, token, n1t, dm, live, qkv, probs, att_t, middle, qkv_full, out_full, up_full, down_full, act, dh, g_up, g_down, up1, down1, own_up, own_down = pl.pallas_call(
            functools.partial(first_kernel, images, slots, width),
            out_shape=[jax.ShapeDtypeStruct(*o) for o in outs],
            in_specs=[VMEM] * 8,
            out_specs=[VMEM] * 2 + [ANY] * 20,
            scratch_shapes=[pltpu.VMEM(*s) for s in scratch]
            + [pltpu.SemaphoreType.DMA((4, 28))] * 2
            + [pltpu.SemaphoreType.DMA((6, 28))] * 2
            + [pltpu.SemaphoreType.DMA((7,))] * 2
            + [pltpu.SemaphoreType.DMA((10,)), pltpu.SemaphoreType.DMA((33,)), pltpu.SemaphoreType.DMA((2,))]
            + [pltpu.SemaphoreType.DMA((4,))] * 2
            + [pltpu.SemaphoreType.DMA((2, 10))] * 2,
            compiler_params=pltpu.CompilerParams(vmem_limit_bytes=LIMIT, collective_id=0, has_side_effects=True),
            name="first",
        )(patches, keep_pad, cotangent, vec, w_qkv, w_out, w_up, w_down)
        final = lambda r, w, lead=(): (lead + (2, 2, r, w), BF16)
        attn = final(48, half)
        outs = [((images, slots, width), F32), ((images, slots, width), BF16), ((part, 3 * width), BF16), ((part, width), BF16), ((part, hidden_width), BF16), ((half, width), BF16), ((16, BLOCK), F32)]

        def buffers(r, w, by_rows, cut, cores, lead, lines):
            other = (4, r - cut, w) if by_rows else (4, r, w - cut)
            first = (4, cut, w) if by_rows else (4, r, cut)
            return [(cores + (4, 2, 2, r, w), BF16)] + [(lead + s, BF16) for s in (other, first, (4, r, w), (4, r, w))] + [(lines + (3, r, w), BF16)]

        scratch = [final(48, THIRD // 2, (3,)), final(width // 4, 128, (3,)), attn, attn, attn, attn]
        scratch += [rows_wide, ((ROWS, TILE), F32), ((ROWS, 3 * width), BF16), heads_like, ((2, H, SLOT, SLOT), BF16), cols_low, cols_low, rows_low, rows_low]
        scratch += [rows_wide, live_like, ((width, 3 * width), BF16), ((width, width), BF16), ((2, slots, width), F32), ((1, 3 * width), F32)] + [row_like] * 6
        scratch += [((4, 4, 2, 2, 2, 48, half), BF16)]
        scratch += [((2, 4, 2, 2, 48, THIRD // 2), BF16), ((4, 48, THIRD // 2), BF16)] + buffers(48, THIRD // 2, False, 128, (), (2,), (3,))
        scratch += [((2, 4, 2, 2, width // 4, 128), BF16), ((4, width // 4, 128), BF16)] + buffers(width // 4, 128, True, 64, (), (2,), (3,))
        scratch += buffers(48, half, False, 128, (4,), (4,), (4,))
        small_like, line_like = ((4, 2, 16, BLOCK), F32), ((3, 16, BLOCK), F32)
        scratch += [small_like, small_like, small_like, ((4, 16, BLOCK), F32), line_like, small_like, small_like]
        grad_patches, out_tokens, o_qkv, o_out, o_up, o_down, small = pl.pallas_call(
            functools.partial(second_kernel, images, slots, width),
            out_shape=[jax.ShapeDtypeStruct(*o) for o in outs],
            in_specs=[VMEM] * 3 + [ANY] * 20,
            out_specs=[ANY] + [VMEM] * 6,
            scratch_shapes=[pltpu.VMEM(*s) for s in scratch]
            + [pltpu.SemaphoreType.DMA((10, 10))] * 2
            + [pltpu.SemaphoreType.DMA((6,))] * 2
            + [pltpu.SemaphoreType.DMA((6,)), pltpu.SemaphoreType.DMA((22,)), pltpu.SemaphoreType.DMA((2,)), pltpu.SemaphoreType.DMA((2,))],
            compiler_params=pltpu.CompilerParams(vmem_limit_bytes=LIMIT, collective_id=1, has_side_effects=True),
            name="second",
        )(keep_pad, vectors, g_b_up, token, n1t, dm, live, qkv, probs, att_t, middle, qkv_full, out_full, up_full, down_full, act, dh, g_up, g_down, up1, down1, own_up, own_down)
        rows = small[:8, :part]
        sum_qkv, sum_out, sum_up, sum_down = (o.astype(F32) for o in (o_qkv, o_out, o_up, o_down))
        b_up_sum = small[8:12, :part].reshape(-1)
    else:
        gather = lambda v: lax.all_gather(v, "fsdp", axis=0, tiled=True)
        vectors = jnp.pad(gather(jnp.concatenate(singles, axis=0).T).T.astype(F32), ((0, 8), (0, 0)))
        bias_up = gather(b_up).astype(F32).reshape(1, hidden_width)
        qkv_full, out_full, up_full, down_full = gather(w_qkv), gather(w_out), gather(w_up), gather(w_down)
        outs = [rows_low, cols_low, rows_low, cols_low, live_like, heads_like, probs_like, cols_low, rows_wide, rows_low, cols_low]
        scratch = [rows_wide, rows_low, mask_like, rows_low, ((1, 3 * width), F32)]
        token, n1t, dm, dmt, live, qkv, probs, att_t, middle, n2, n2t = call(
            functools.partial(first_plain, images, slots, width),
            outs, scratch, (patches, keep_pad, cotangent, vectors, qkv_full, out_full), "first",
        )
        gain1, gain2, b_d = vectors[0:1], vectors[5:6], vectors[7:8]
        hid = ((ROWS, hidden_width), BF16)
        out_tokens, d_mid, d_low, g_up, g_down, g_b_up, g_g2, g_s2, g_bd, g_bo = call(
            functools.partial(second_plain, images, slots, width, hidden_width),
            [((images, slots, width), BF16), rows_wide, rows_low] + [((width, hidden_width), BF16)] * 2 + [((1, hidden_width), F32)] + [row_like] * 4,
            [hid, hid, rows_wide],
            (n2, n2t, dm, dmt, up_full, bias_up, down_full, b_d, middle, live, gain2),
            "second",
        )
        g_out, g_qkv, g_b, g_g1, g_s1, grad_patches = call(
            functools.partial(third_plain, images, slots, width),
            [((width, width), BF16), ((width, 3 * width), BF16), ((1, 3 * width), F32), row_like, row_like, ((images, slots, width), F32)],
            [rows_wide, ((ROWS, TILE), F32), ((ROWS, 3 * width), BF16), heads_like],
            (d_low, att_t, out_full, qkv, probs, n1t, qkv_full, token, gain1, d_mid, live, keep_pad),
            "third",
        )
        scat = lambda v, dim=0: lax.psum(lax.psum_scatter(v, "fsdp", scatter_dimension=dim, tiled=True), "dp").astype(F32)
        rows = jnp.concatenate([g_g1, g_s1, g_b[:, :width], g_b[:, 2 * width :], g_bo, g_g2, g_s2, g_bd], axis=0).astype(BF16)
        rows = scat(rows, 1)
        b_up_sum = scat(g_b_up.astype(BF16), 1)[0]
        sum_qkv, sum_out, sum_up, sum_down = scat(g_qkv), scat(g_out), scat(g_up), scat(g_down, 1).T
    return (
        out_tokens, grad_patches, rows[0], rows[1], sum_qkv, rows[2], rows[3], sum_out, rows[4],
        rows[5], rows[6], sum_up, b_up_sum, sum_down, rows[7],
    )


def solution(mesh):
    linked = (mesh.shape["fsdp"], mesh.shape["dp"]) == (8, 4)
    many, one, two = P(("fsdp", "dp"), None, None), P("fsdp"), P("fsdp", None)
    in_specs = (many, P(("fsdp", "dp"), None), one, one, two, one, one, two, one, one, one, two, one, two, one, many)
    out_specs = (many, many, one, one, two, one, one, two, one, one, one, two, one, two, one)
    return jax.shard_map(functools.partial(shards, linked), mesh=mesh, in_specs=in_specs, out_specs=out_specs, check_vma=False)
```

profile of v0, /device:TPU:1, one launch (start us, length us, event | category | flops | bytes accessed | tf_op | source)
XLA Modules:
  0.0 198.1 jit_solution(10870453934604251132)
XLA Ops:
  0.6 0.8 reshape.72
  1.4 0.8 concatenate.3
  2.2 0.6 pad.9.vec
  2.8 0.7 pad.8
  3.5 0.6 reshape.63.keep
  4.1 102.3 %first.1 = (f32[16,768]{1,0:T(8,128)}, f32[3,1,1024]{2,1,0:T(1,128)}, bf16[1024,768]{1,0:T(8,128)(2,1)}, bf16[768,1024]{1,0:T(8,128)(2,1)}, bf16[1024,768]{1,0:T...) custom-call(bf16[5,197,768]{2,1,0:T(8,128)(2,1)} %patches.1, ...), custom_call_target="tpu_custom_call" | custom-call | tf_op jit(solution)/shard_map/first/pallas_call | solution.py:1216
  106.4 78.8 %second.1 = (f32[5,197,768]{2,1,0:T(8,128)}, bf16[5,197,768]{2,1,0:T(8,128)(2,1)}, bf16[96,2304]{1,0:T(8,128)(2,1)}, bf16[96,768]{1,0:T(8,128)(2,1)}, bf16[96,30...) custom-call(s32[5,1,200]{2,1,0:T(1,128)} %reshape.63.keep, f32[16,768]{1,0:T(8,128)} %get-tuple-element.44.vectors, ...), custom_call_target="tpu_custom_call" | custom-call | tf_op jit(solution)/shard_map/second/pallas_call | solution.py:1249
  185.2 0.0 copy-start.3
  185.2 0.7 slice.43
  185.9 1.5 slice_bitcast_fusion
  187.4 0.7 reshape.73
  188.1 1.6 convert_element_type.15
  189.8 0.0 copy-start.2
  189.8 2.0 %convert_element_type.14 = f32[96,2304]{1,0:T(8,128)} convert(bf16[96,2304]{1,0:T(8,128)(2,1)} %get-tuple-element.69) | non-fusion elementwise | flops 221184 | bytes 1327104 | tf_op jit(solution)/shard_map/convert_element_type | solution.py:1262
  191.8 0.0 copy-done.3
  191.8 0.0 copy-start.1
  191.8 1.1 convert_element_type.16
  192.9 0.0 copy-done.2
  192.9 1.1 convert_element_type.17
  194.0 0.0 copy-done.1
  194.0 0.0 copy-start
  194.0 1.1 copy.33
  195.1 1.3 copy-done
  196.4 1.6 copy.34
Async XLA Ops:
  185.2 6.6 %copy-start.3 = (bf16[96,3072]{1,0:T(8,128)(2,1)S(1)}, bf16[96,3072]{1,0:T(8,128)(2,1)}, u32[]{:S(2)}) copy-start(bf16[96,3072]{1,0:T(8,128)(2,1)} %get-tuple-element.71) | copy-start | bytes 1769476
  189.8 3.2 %copy-start.2 = (bf16[384,768]{1,0:T(8,128)(2,1)S(1)}, bf16[384,768]{1,0:T(8,128)(2,1)}, u32[]{:S(2)}) copy-start(bf16[384,768]{1,0:T(8,128)(2,1)} %get-tuple-element.72) | copy-start | bytes 1769476
  191.8 2.2 %copy-start.1 = (bf16[5,197,768]{2,1,0:T(8,128)(2,1)S(1)}, bf16[5,197,768]{2,1,0:T(8,128)(2,1)}, u32[]{:S(2)}) copy-start(bf16[5,197,768]{2,1,0:T(8,128)(2,1)} %get-tuple-element.96) | copy-start | bytes 4538884
  194.0 2.4 %copy-start = (f32[5,197,768]{2,1,0:T(8,128)S(1)}, f32[5,197,768]{2,1,0:T(8,128)}, u32[]{:S(2)}) copy-start(f32[5,197,768]{2,1,0:T(8,128)} %get-tuple-element.97) | copy-start | bytes 9077764
where the time goes:
time: 198 us
  Pallas kernels  181 us (91%)
  local copies, waits for them, and re-layouts  10.5 us (5%)
  other arithmetic  5.89 us (3%)
    pallas_call x1, Pallas kernels, shards(): pl.pallas_call(functools.partial(first_kernel, images, slots, width), out...  102 us
    pallas_call x1, Pallas kernels, shards(): pl.pallas_call(functools.partial(second_kernel, images, slots, width), ou...  78.8 us
    convert_element_type x4, other arithmetic, shards(): o.astype(F32)  5.89 us
    unnamed x10, local copies, waits for them, and re-layouts  4.07 us

commit v1 on v0

--- a/solution.py
+++ b/solution.py
@@ -76,6 +76,12 @@
 
 def first_lanes(rows):
     return lax.broadcasted_iota(jnp.int32, (rows, 2 * HD), 1) < HD
+
+
+def pad_keep(keep, padded):
+    padded[...] = jnp.full_like(padded, -1)
+    for i in range(keep.shape[0]):
+        padded[i, :, : keep.shape[1]] = keep[i : i + 1, :]
 
 
 def stage_gather(images, slots, patches, keep, stack, live, mask, token):
@@ -190,16 +196,22 @@
 
 def stage_mlp(width, normed, normed_t, dm, dm_t, w_up, b_up, w_down, act, dh, put_up, put_down, g_b_up, c):
     cols = tile_at(c, TILE)
-    hidden = dot(normed[...], w_up[:, cols]) + b_up[:, cols]
-    d_act = dot_nt(dm[...], w_down[cols, :])
-    value, slope = gelu_parts(hidden)
-    value = value.astype(BF16)
-    grad = (d_act * slope).astype(BF16)
-    act[:, cols] = value
-    dh[:, cols] = grad
-    g_b_up[:, cols] = jnp.sum(grad.astype(F32), axis=0, keepdims=True)
-    put_up(c, dot(normed_t[...], grad).astype(BF16))
-    put_down(c, dot(dm_t[...], value).astype(BF16))
+    up, down, bias = w_up[:, cols], w_down[cols, :], b_up[:, cols]
+    total, waiting = 0.0, []
+    for r in range(ROWS // TILE + 1):
+        if r < ROWS // TILE:
+            rows = slice(r * TILE, (r + 1) * TILE)
+            waiting.append((rows, dot(normed[rows, :], up) + bias, dot_nt(dm[rows, :], down)))
+        if r:
+            rows, hidden, d_act = waiting.pop(0)
+            value, slope = gelu_parts(hidden)
+            grad = (d_act * slope).astype(BF16)
+            act[rows, cols] = value.astype(BF16)
+            dh[rows, cols] = grad
+            total = total + jnp.sum(grad.astype(F32), axis=0, keepdims=True)
+    g_b_up[:, cols] = total
+    put_up(c, dot(normed_t[...], dh[:, cols]).astype(BF16))
+    put_down(c, dot(dm_t[...], act[:, cols]).astype(BF16))
 
 
 def add_products(width, stack, fresh, product):
@@ -670,13 +682,13 @@
 )
 MERGE_PLAN = (22, 25, 26)
 REDUCE_PLAN = (
-    ("m0", (5, 21)),
-    ("m1", (0, 4, 9, 14, 22)),
-    ("m2", (2, 8, 13, 19, 21)),
-    ("o", (7, 12, 15, 20, 21)),
-    ("q", (13, 15, 17, 19, 21)),
-    ("k", (14, 16, 19, 21, 21)),
-    ("v", (14, 18, 19, 21, 22)),
+    ("m0", (13, 14)),
+    ("m1", (0, 4, 10, 20, 22)),
+    ("m2", (3, 8, 13, 20, 22)),
+    ("o", (12, 15, 18, 20, 22)),
+    ("q", (13, 14, 16, 19, 21)),
+    ("k", (14, 16, 19, 22, 22)),
+    ("v", (14, 18, 20, 22, 22)),
 )
 
 
@@ -735,23 +747,43 @@
 
 def first_kernel(
     images, slots, width,
-    patches, keep, cot, vec, s_qkv, s_out, s_up, s_down,
+    h_patches, keep_in, h_cot, *rest,
+):
+    singles, rest = rest[:9], rest[9:]
+    first_body(images, slots, width, h_patches, keep_in, h_cot, singles, *rest)
+
+
+def first_body(
+    images, slots, width,
+    h_patches, keep_in, h_cot, singles, s_qkv, s_out, s_up, s_down,
     vectors, g_b_up, h_token, h_n1t, h_dm, h_live, h_qkv, h_probs, h_att_t, h_middle, h_wqkv, h_wout, h_up, h_down, h_act, h_dh, h_gup, h_gdown, h_up1, h_down1, h_own_up, h_own_down,
-    stack, normed, mask, token, n1t, dm, dmt, live, qkv, probs, att_t, middle, f_qkv, f_out, f_up, f_down, s_up3, act_, dh, g_up, g_down, up_core, down_core, up_dx, up_dy, up_sx, up_sy, dn_dx, dn_dy, dn_sx, dn_sy,
+    patches, keep, cot, vec_wide, vec, stack, normed, mask, token, n1t, dm, dmt, live, qkv, probs, att_t, middle, f_qkv, f_out, f_up, f_down, s_up3, act_, dh, g_up, g_down, up_core, down_core, up_dx, up_dy, up_sx, up_sy, dn_dx, dn_dy, dn_sx, dn_sy,
     vecs, bias, b_up, q_send, q_recv, m_send, m_recv, v_send, v_recv, own, saves, probs_sem, r_send, r_recv, w_send, w_recv,
 ):
     place = Place()
     _, side_y, side_c = place.sides()
     flat = [place.to(z=place.zs[k], x=x) for k in range(4) for x in (place.x, place.ox)][1:]
     later = Later(saves)
+    loads = [pltpu.make_async_copy(h_patches, patches, own.at[10]), pltpu.make_async_copy(h_cot, cot, own.at[11])]
 
     def before():
+        for load in loads:
+            load.start()
+        pad_keep(keep_in, keep)
+        vec_wide[...] = jnp.zeros_like(vec_wide)
+        for j in range(8):
+            vec_wide[j : j + 1, :96] = singles[j][...].astype(F32)
+        for j in range(4):
+            vec_wide[8 + j : 9 + j, :96] = singles[8][:, 96 * j : 96 * j + 96].astype(F32)
+        vec[...] = vec_wide[...].astype(BF16)
+        loads[0].wait()
         for t in range(3):
             for f in range(8):
                 s_up3[t, :, f * 128 : f * 128 + 128] = s_up[:, f * 384 + t * 128 : f * 384 + t * 128 + 128]
         stage_gather(images, slots, patches, keep, stack, live, mask, token)
         later.start("live", live, h_live)
         later.start("token", token, h_token)
+        loads[1].wait()
         stage_grads(images, slots, width, cot, stack, live, dm, dmt)
         later.start("dm", dm, h_dm)
 
@@ -976,8 +1008,9 @@
 
 def second_kernel(
     images, slots, width,
-    keep, vectors, s_bup, h_token, h_n1t, h_dm, h_live, h_qkv, h_probs, h_att_t, h_middle, h_wqkv, h_wout, h_up, h_down, h_act, h_dh, h_gup, h_gdown, h_up1, h_down1, h_own_up, h_own_down,
-    gp, out_tokens, o_qkv, o_out, o_up, o_down, e_small,
+    keep_in, vectors, s_bup, h_token, h_n1t, h_dm, h_live, h_qkv, h_probs, h_att_t, h_middle, h_wqkv, h_wout, h_up, h_down, h_act, h_dh, h_gup, h_gdown, h_up1, h_down1, h_own_up, h_own_down,
+    gp, out_tokens, o_wide, o_down, e_small,
+    out_vm, keep,
     e_up, e_down, e_out, e_q, e_k, e_v,
     stack, tile, flat, qkv, probs, t_a, t_b, r_a, r_b, mid, live, w_qkv, w_out, stage, g_b, g_g1, g_s1, g_g2, g_s2, g_bd, g_bo, g_attn,
     up_held, up_own, up_core, up_dx, up_dy, up_sx, up_sy, up_ln, dn_held, dn_own, dn_core, dn_dx, dn_dy, dn_sx, dn_sy, dn_ln,
@@ -985,6 +1018,7 @@
     send, recv, v_send, v_recv, own, loads, probs_sem, out_sem,
 ):
     place = Place()
+    pad_keep(keep_in, keep)
     enter(place.along[1:] + list(place.sides()))
     def reduce_third(t, source, held, own4, core, dx, dy, sx, sy, ln, e, sem):
         sems = send.at[sem + t], recv.at[sem + t]
@@ -1143,7 +1177,8 @@
     add_products(width, stack, False, lambda cols: dot(slots_[0][...], r_b[:, cols]))
     small.step_x(v_total)
     act(20)
-    stage_final(images, slots, width, mid, live, vectors.at[7:8, :], stack, out_tokens)
+    stage_final(images, slots, width, mid, live, vectors.at[7:8, :], stack, out_vm)
+    later.start("tokens", out_vm, out_tokens)
     small.step_line(e_small)
     act(21)
     act(22)
@@ -1154,7 +1189,7 @@
             for y in range(2):
                 for f in range(4):
                     col = (4 * y + f) * 384 + t * 128
-                    o_up[48 * c : 48 * c + 48, col : col + 128] = e_up[t, c, y, :, f * 128 : f * 128 + 128]
+                    o_wide[48 * c : 48 * c + 48, 3 * width + col : 3 * width + col + 128] = e_up[t, c, y, :, f * 128 : f * 128 + 128]
         o_down[t * 128 : t * 128 + 128, :] = e_down[t].reshape(width, 128).T
     half = width // 2
 
@@ -1164,14 +1199,37 @@
                 ref[48 * c : 48 * c + 48, base + y * half : base + y * half + half] = e[c, y]
 
     r_out.finish()
-    place_blocks(o_out, 0, e_out)
+    place_blocks(o_wide, 7 * width, e_out)
     for m, (r, e) in enumerate(((r_q, e_q), (r_k, e_k), (r_v, e_v))):
         r.finish()
-        place_blocks(o_qkv, m * width, e)
+        place_blocks(o_wide, m * width, e)
+    later.wait("tokens")
     for copy in flights[-2:]:
         copy.wait()
     for r in r_up + r_down + [r_out, r_q, r_k, r_v, small]:
         r.drain()
+
+
+def last_kernel(images, width, h_patches, h_tokens, small, wide, down, patches, tokens, o_qkv, o_up, o_out, o_down, o_b_up, *rest):
+    vectors, (held_p, held_t, loads, stores) = rest[:8], rest[8:]
+    copies = []
+    for i in range(images):
+        for j, (src, held, dst) in enumerate(((h_patches, held_p, patches), (h_tokens, held_t, tokens))):
+            load = pltpu.make_async_copy(src.at[i], held.at[i], loads.at[2 * i + j])
+            load.start()
+            copies.append((load, pltpu.make_async_copy(held.at[i], dst.at[i], stores.at[2 * i + j])))
+    for load, store in copies:
+        load.wait()
+        store.start()
+    o_qkv[...] = wide[:, : 3 * width].astype(F32)
+    o_up[...] = wide[:, 3 * width : 7 * width].astype(F32)
+    o_out[...] = wide[:, 7 * width :].astype(F32)
+    o_down[...] = down[...].astype(F32)
+    for j, ref in enumerate(vectors):
+        ref[...] = small[j : j + 1, :96]
+    o_b_up[...] = jnp.concatenate([small[8 + j : 9 + j, :96] for j in range(4)], axis=1)
+    for _, store in copies:
+        store.wait()
 
 
 def shards(
@@ -1194,8 +1252,6 @@
 
     if linked:
         half = width // 2
-        vec = jnp.concatenate(singles + [b_up.reshape(4, part)], axis=0)
-        vec = jnp.pad(vec, ((0, 4), (0, BLOCK - part)))
         full = lambda v: ((v.shape[0] * 8, v.shape[1]), BF16)
         up3, down3, hid3 = ((3, width, THIRD), BF16), ((3, THIRD, width), BF16), ((3, ROWS, THIRD), BF16)
         gup_like, gdown_like = (4, 2, 2, 2, 48, THIRD // 2), (4, 2, 2, 2, width // 4, 128)
@@ -1205,6 +1261,7 @@
             ((4,) + gup_like[4:], BF16), ((4,) + gdown_like[4:], BF16),
         ]
         scratch = [
+            (patches.shape, BF16), ((images, 1, SLOT), jnp.int32), (patches.shape, BF16), ((16, BLOCK), F32), ((16, BLOCK), BF16),
             rows_wide, rows_low, mask_like, rows_low, cols_low, rows_low, cols_low, live_like, heads_like, ((2, H, SLOT, SLOT), BF16), cols_low,
             rows_wide, full(w_qkv), full(w_out), up3, down3, ((3, part, THIRD), BF16), hid3[0][1:], hid3[0][1:], (2,) + gup_like, (2,) + gdown_like,
             (2, 4, 2) + gup_like[3:], (2, 4, 2) + gdown_like[3:],
@@ -1216,28 +1273,28 @@
         vectors, g_b_up, token, n1t, dm, live, qkv, probs, att_t, middle, qkv_full, out_full, up_full, down_full, act, dh, g_up, g_down, up1, down1, own_up, own_down = pl.pallas_call(
             functools.partial(first_kernel, images, slots, width),
             out_shape=[jax.ShapeDtypeStruct(*o) for o in outs],
-            in_specs=[VMEM] * 8,
+            in_specs=[ANY, VMEM, ANY] + [VMEM] * 13,
             out_specs=[VMEM] * 2 + [ANY] * 20,
             scratch_shapes=[pltpu.VMEM(*s) for s in scratch]
             + [pltpu.SemaphoreType.DMA((4, 28))] * 2
             + [pltpu.SemaphoreType.DMA((6, 28))] * 2
             + [pltpu.SemaphoreType.DMA((7,))] * 2
-            + [pltpu.SemaphoreType.DMA((10,)), pltpu.SemaphoreType.DMA((33,)), pltpu.SemaphoreType.DMA((2,))]
+            + [pltpu.SemaphoreType.DMA((12,)), pltpu.SemaphoreType.DMA((33,)), pltpu.SemaphoreType.DMA((2,))]
             + [pltpu.SemaphoreType.DMA((4,))] * 2
             + [pltpu.SemaphoreType.DMA((2, 10))] * 2,
             compiler_params=pltpu.CompilerParams(vmem_limit_bytes=LIMIT, collective_id=0, has_side_effects=True),
             name="first",
-        )(patches, keep_pad, cotangent, vec, w_qkv, w_out, w_up, w_down)
+        )(patches, keep, cotangent, *singles, b_up.reshape(1, -1), w_qkv, w_out, w_up, w_down)
         final = lambda r, w, lead=(): (lead + (2, 2, r, w), BF16)
         attn = final(48, half)
-        outs = [((images, slots, width), F32), ((images, slots, width), BF16), ((part, 3 * width), BF16), ((part, width), BF16), ((part, hidden_width), BF16), ((half, width), BF16), ((16, BLOCK), F32)]
+        outs = [((images, slots, width), F32), ((images, slots, width), BF16), ((part, 8 * width), BF16), ((half, width), BF16), ((16, BLOCK), F32)]
 
         def buffers(r, w, by_rows, cut, cores, lead, lines):
             other = (4, r - cut, w) if by_rows else (4, r, w - cut)
             first = (4, cut, w) if by_rows else (4, r, cut)
             return [(cores + (4, 2, 2, r, w), BF16)] + [(lead + s, BF16) for s in (other, first, (4, r, w), (4, r, w))] + [(lines + (3, r, w), BF16)]
 
-        scratch = [final(48, THIRD // 2, (3,)), final(width // 4, 128, (3,)), attn, attn, attn, attn]
+        scratch = [((images, slots, width), BF16), ((images, 1, SLOT), jnp.int32), final(48, THIRD // 2, (3,)), final(width // 4, 128, (3,)), attn, attn, attn, attn]
         scratch += [rows_wide, ((ROWS, TILE), F32), ((ROWS, 3 * width), BF16), heads_like, ((2, H, SLOT, SLOT), BF16), cols_low, cols_low, rows_low, rows_low]
         scratch += [rows_wide, live_like, ((width, 3 * width), BF16), ((width, width), BF16), ((2, slots, width), F32), ((1, 3 * width), F32)] + [row_like] * 6
         scratch += [((4, 4, 2, 2, 2, 48, half), BF16)]
@@ -1246,21 +1303,33 @@
         scratch += buffers(48, half, False, 128, (4,), (4,), (4,))
         small_like, line_like = ((4, 2, 16, BLOCK), F32), ((3, 16, BLOCK), F32)
         scratch += [small_like, small_like, small_like, ((4, 16, BLOCK), F32), line_like, small_like, small_like]
-        grad_patches, out_tokens, o_qkv, o_out, o_up, o_down, small = pl.pallas_call(
+        grad_patches, out_tokens, o_wide, o_down, small = pl.pallas_call(
             functools.partial(second_kernel, images, slots, width),
             out_shape=[jax.ShapeDtypeStruct(*o) for o in outs],
             in_specs=[VMEM] * 3 + [ANY] * 20,
-            out_specs=[ANY] + [VMEM] * 6,
+            out_specs=[ANY] * 2 + [VMEM] * 3,
             scratch_shapes=[pltpu.VMEM(*s) for s in scratch]
             + [pltpu.SemaphoreType.DMA((10, 10))] * 2
             + [pltpu.SemaphoreType.DMA((6,))] * 2
-            + [pltpu.SemaphoreType.DMA((6,)), pltpu.SemaphoreType.DMA((22,)), pltpu.SemaphoreType.DMA((2,)), pltpu.SemaphoreType.DMA((2,))],
+            + [pltpu.SemaphoreType.DMA((6,)), pltpu.SemaphoreType.DMA((23,)), pltpu.SemaphoreType.DMA((2,)), pltpu.SemaphoreType.DMA((2,))],
             compiler_params=pltpu.CompilerParams(vmem_limit_bytes=LIMIT, collective_id=1, has_side_effects=True),
             name="second",
-        )(keep_pad, vectors, g_b_up, token, n1t, dm, live, qkv, probs, att_t, middle, qkv_full, out_full, up_full, down_full, act, dh, g_up, g_down, up1, down1, own_up, own_down)
-        rows = small[:8, :part]
-        sum_qkv, sum_out, sum_up, sum_down = (o.astype(F32) for o in (o_qkv, o_out, o_up, o_down))
-        b_up_sum = small[8:12, :part].reshape(-1)
+        )(keep, vectors, g_b_up, token, n1t, dm, live, qkv, probs, att_t, middle, qkv_full, out_full, up_full, down_full, act, dh, g_up, g_down, up1, down1, own_up, own_down)
+        outs = [
+            ((images, slots, width), F32), ((images, slots, width), BF16), ((part, 3 * width), F32), ((part, 4 * width), F32), ((part, width), F32),
+            ((half, width), F32), ((1, half), F32),
+        ] + [((1, part), F32)] * 8
+        grad_patches, out_tokens, sum_qkv, sum_up, sum_out, sum_down, b_up_sum, *rows = pl.pallas_call(
+            functools.partial(last_kernel, images, width),
+            out_shape=[jax.ShapeDtypeStruct(*o) for o in outs],
+            in_specs=[ANY, ANY, VMEM, VMEM, VMEM],
+            out_specs=[ANY, ANY] + [VMEM] * 13,
+            scratch_shapes=[pltpu.VMEM((images, slots, width), F32), pltpu.VMEM((images, slots, width), BF16)] + [pltpu.SemaphoreType.DMA((2 * images,))] * 2,
+            compiler_params=pltpu.CompilerParams(vmem_limit_bytes=LIMIT),
+            name="last",
+        )(grad_patches, out_tokens, small, o_wide, o_down)
+        rows = [row.reshape(part) for row in rows]
+        b_up_sum = b_up_sum.reshape(half)
     else:
         gather = lambda v: lax.all_gather(v, "fsdp", axis=0, tiled=True)
         vectors = jnp.pad(gather(jnp.concatenate(singles, axis=0).T).T.astype(F32), ((0, 8), (0, 0)))

time: 198 us -> 190 us (0.960)
  local copies, waits for them, and re-layouts: 10.5 us -> 1.24 us
  Pallas kernels: 181 us -> 186 us
  other arithmetic: 5.89 us -> 1.27 us
    pallas_call x0 -> x1, Pallas kernels: none -> 7.13 us  [shards(): pl.pallas_call(functools.partial(last_kernel, images, width), out_shape=[...]
    convert_element_type x4 -> x0, other arithmetic: 5.89 us -> none  [shards(): o.astype(F32)]
    unnamed x10 -> x0, local copies, waits for them, and re-layouts: 4.07 us -> none
where the time goes in v1:
time: 190 us
  Pallas kernels  186 us (98%)
    pallas_call x1, Pallas kernels, shards(): pl.pallas_call(functools.partial(first_kernel, images, slots, width), out...  101 us
    pallas_call x1, Pallas kernels, shards(): pl.pallas_call(functools.partial(second_kernel, images, slots, width), ou...  77.9 us
    pallas_call x1, Pallas kernels, shards(): pl.pallas_call(functools.partial(last_kernel, images, width), out_shape=[...  7.13 us

profile of v1, /device:TPU:1, one launch (start us, length us, event | category | flops | bytes accessed | tf_op | source)
XLA Modules:
  0.0 189.6 jit_solution(2155346963190737368)
XLA Ops:
  0.6 1.2 reshape.92.rest_8_
  1.9 101.4 %first.1 = (f32[16,768]{1,0:T(8,128)}, f32[3,1,1024]{2,1,0:T(1,128)}, bf16[1024,768]{1,0:T(8,128)(2,1)}, bf16[768,1024]{1,0:T(8,128)(2,1)}, bf16[1024,768]{1,0:T...) custom-call(bf16[5,197,768]{2,1,0:T(8,128)(2,1)} %h_patches.1, ...), custom_call_target="tpu_custom_call" | custom-call | tf_op jit(solution)/shard_map/first/pallas_call | solution.py:1273
  103.3 77.9 %second.1 = (f32[5,197,768]{2,1,0:T(8,128)}, bf16[5,197,768]{2,1,0:T(8,128)(2,1)}, bf16[96,6144]{1,0:T(8,128)(2,1)}, bf16[384,768]{1,0:T(8,128)(2,1)}, f32[16,128]{1,0:T(8,128)}) custom-call(s32[5,197]{1,0:T(8,128)} %keep_in.3, f32[16,768]{1,0:T(8,128)} %get-tuple-element.57.vectors, f32[3,1,1024]{2,1,0:T(1,128)} %get-tuple-element.58.s_bup, ...), custom_call_target="tpu_custom_call" | custom-call | tf_op jit(solution)/shard_map/second/pallas_call | solution.py:1306
  181.2 7.1 %last.1 = (f32[5,197,768]{2,1,0:T(8,128)}, bf16[5,197,768]{2,1,0:T(8,128)(2,1)}, f32[96,2304]{1,0:T(8,128)}, f32[96,3072]{1,0:T(8,128)}, f32[96,768]{1,0:T(8,128...) custom-call(f32[5,197,768]{2,1,0:T(8,128)} %get-tuple-element.79.h_p, ...), custom_call_target="tpu_custom_call" | custom-call | tf_op jit(solution)/shard_map/last/pallas_call | solution.py:1322
  188.3 1.3 reduce

commit v2 on v1

--- a/solution.py
+++ b/solution.py
@@ -773,8 +773,9 @@
         vec_wide[...] = jnp.zeros_like(vec_wide)
         for j in range(8):
             vec_wide[j : j + 1, :96] = singles[j][...].astype(F32)
+        row = jnp.concatenate([singles[8][...].astype(F32)[j : j + 1] for j in range(3)], axis=1)
         for j in range(4):
-            vec_wide[8 + j : 9 + j, :96] = singles[8][:, 96 * j : 96 * j + 96].astype(F32)
+            vec_wide[8 + j : 9 + j, :96] = row[:, 96 * j : 96 * j + 96]
         vec[...] = vec_wide[...].astype(BF16)
         loads[0].wait()
         for t in range(3):
@@ -1210,25 +1211,37 @@
         r.drain()
 
 
-def last_kernel(images, width, h_patches, h_tokens, small, wide, down, patches, tokens, o_qkv, o_up, o_out, o_down, o_b_up, *rest):
-    vectors, (held_p, held_t, loads, stores) = rest[:8], rest[8:]
+def last_kernel(images, width, h_patches, h_tokens, small, h_wide, h_down, patches, tokens, o_qkv, o_up, o_out, o_down, o_b_up, *rest):
+    vectors, (held_p, held_t, wide, down, f_wide, f_down, loads, stores, own) = rest[:8], rest[8:]
+    first = [pltpu.make_async_copy(h_wide, wide, own.at[0]), pltpu.make_async_copy(h_down, down, own.at[1])]
+    for load in first:
+        load.start()
     copies = []
     for i in range(images):
         for j, (src, held, dst) in enumerate(((h_patches, held_p, patches), (h_tokens, held_t, tokens))):
             load = pltpu.make_async_copy(src.at[i], held.at[i], loads.at[2 * i + j])
             load.start()
             copies.append((load, pltpu.make_async_copy(held.at[i], dst.at[i], stores.at[2 * i + j])))
+    for j, ref in enumerate(vectors):
+        ref[...] = small[j : j + 1, :96]
+    row = jnp.concatenate([small[8 + j : 9 + j, :96] for j in range(4)], axis=1)
+    for j in range(3):
+        o_b_up[j : j + 1, :] = row[:, j * 128 : (j + 1) * 128]
+    stored = []
+    first[1].wait()
+    f_down[...] = down[...].astype(F32)
+    stored.append(pltpu.make_async_copy(f_down, o_down, own.at[2]))
+    stored[-1].start()
+    first[0].wait()
+    for j, (dst, begin, end) in enumerate(((o_qkv, 0, 3), (o_up, 3, 7), (o_out, 7, 8))):
+        cols = slice(begin * width, end * width)
+        f_wide[:, cols] = wide[:, cols].astype(F32)
+        stored.append(pltpu.make_async_copy(f_wide.at[:, cols], dst, own.at[3 + j]))
+        stored[-1].start()
     for load, store in copies:
         load.wait()
         store.start()
-    o_qkv[...] = wide[:, : 3 * width].astype(F32)
-    o_up[...] = wide[:, 3 * width : 7 * width].astype(F32)
-    o_out[...] = wide[:, 7 * width :].astype(F32)
-    o_down[...] = down[...].astype(F32)
-    for j, ref in enumerate(vectors):
-        ref[...] = small[j : j + 1, :96]
-    o_b_up[...] = jnp.concatenate([small[8 + j : 9 + j, :96] for j in range(4)], axis=1)
-    for _, store in copies:
+    for store in stored + [store for _, store in copies]:
         store.wait()
 
 
@@ -1284,7 +1297,7 @@
             + [pltpu.SemaphoreType.DMA((2, 10))] * 2,
             compiler_params=pltpu.CompilerParams(vmem_limit_bytes=LIMIT, collective_id=0, has_side_effects=True),
             name="first",
-        )(patches, keep, cotangent, *singles, b_up.reshape(1, -1), w_qkv, w_out, w_up, w_down)
+        )(patches, keep, cotangent, *singles, b_up.reshape(3, -1), w_qkv, w_out, w_up, w_down)
         final = lambda r, w, lead=(): (lead + (2, 2, r, w), BF16)
         attn = final(48, half)
         outs = [((images, slots, width), F32), ((images, slots, width), BF16), ((part, 8 * width), BF16), ((half, width), BF16), ((16, BLOCK), F32)]
@@ -1317,14 +1330,19 @@
         )(keep, vectors, g_b_up, token, n1t, dm, live, qkv, probs, att_t, middle, qkv_full, out_full, up_full, down_full, act, dh, g_up, g_down, up1, down1, own_up, own_down)
         outs = [
             ((images, slots, width), F32), ((images, slots, width), BF16), ((part, 3 * width), F32), ((part, 4 * width), F32), ((part, width), F32),
-            ((half, width), F32), ((1, half), F32),
+            ((half, width), F32), ((3, 128), F32),
         ] + [((1, part), F32)] * 8
         grad_patches, out_tokens, sum_qkv, sum_up, sum_out, sum_down, b_up_sum, *rows = pl.pallas_call(
             functools.partial(last_kernel, images, width),
             out_shape=[jax.ShapeDtypeStruct(*o) for o in outs],
-            in_specs=[ANY, ANY, VMEM, VMEM, VMEM],
-            out_specs=[ANY, ANY] + [VMEM] * 13,
-            scratch_shapes=[pltpu.VMEM((images, slots, width), F32), pltpu.VMEM((images, slots, width), BF16)] + [pltpu.SemaphoreType.DMA((2 * images,))] * 2,
+            in_specs=[ANY, ANY, VMEM, ANY, ANY],
+            out_specs=[ANY] * 6 + [VMEM] * 9,
+            scratch_shapes=[
+                pltpu.VMEM(*s)
+                for s in (((images, slots, width), F32), ((images, slots, width), BF16), ((part, 8 * width), BF16), ((half, width), BF16), ((part, 8 * width), F32), ((half, width), F32))
+            ]
+            + [pltpu.SemaphoreType.DMA((2 * images,))] * 2
+            + [pltpu.SemaphoreType.DMA((6,))],
             compiler_params=pltpu.CompilerParams(vmem_limit_bytes=LIMIT),
             name="last",
         )(grad_patches, out_tokens, small, o_wide, o_down)

time: 190 us -> 188 us (0.989)
  no operation moved by 1% of the time
where the time goes in v2:
time: 188 us
  Pallas kernels  187 us (99%)
    pallas_call x1, Pallas kernels, shards(): pl.pallas_call(functools.partial(first_kernel, images, slots, width), out...  101 us
    pallas_call x1, Pallas kernels, shards(): pl.pallas_call(functools.partial(second_kernel, images, slots, width), ou...  77.8 us
    pallas_call x1, Pallas kernels, shards(): pl.pallas_call(functools.partial(last_kernel, images, width), out_shape=[...  7.53 us

profile of v2, /device:TPU:1, one launch (start us, length us, event | category | flops | bytes accessed | tf_op | source)
XLA Modules:
  0.0 187.5 jit_solution(13991082130746477133)
XLA Ops:
  0.7 101.3 %first.1 = (f32[16,768]{1,0:T(8,128)}, f32[3,1,1024]{2,1,0:T(1,128)}, bf16[1024,768]{1,0:T(8,128)(2,1)}, bf16[768,1024]{1,0:T(8,128)(2,1)}, bf16[1024,768]{1,0:T...) custom-call(bf16[5,197,768]{2,1,0:T(8,128)(2,1)} %h_patches.1, ...), custom_call_target="tpu_custom_call" | custom-call | tf_op jit(solution)/shard_map/first/pallas_call | solution.py:1286
  102.0 77.8 %second.1 = (f32[5,197,768]{2,1,0:T(8,128)}, bf16[5,197,768]{2,1,0:T(8,128)(2,1)}, bf16[96,6144]{1,0:T(8,128)(2,1)}, bf16[384,768]{1,0:T(8,128)(2,1)}, f32[16,128]{1,0:T(8,128)}) custom-call(s32[5,197]{1,0:T(8,128)} %keep_in.3, f32[16,768]{1,0:T(8,128)} %get-tuple-element.57.vectors, f32[3,1,1024]{2,1,0:T(1,128)} %get-tuple-element.58.s_bup, ...), custom_call_target="tpu_custom_call" | custom-call | tf_op jit(solution)/shard_map/second/pallas_call | solution.py:1319
  179.8 7.5 %last.1 = (f32[5,197,768]{2,1,0:T(8,128)}, bf16[5,197,768]{2,1,0:T(8,128)(2,1)}, f32[96,2304]{1,0:T(8,128)}, f32[96,3072]{1,0:T(8,128)}, f32[96,768]{1,0:T(8,128...) custom-call(f32[5,197,768]{2,1,0:T(8,128)} %get-tuple-element.79.h_p, ...), custom_call_target="tpu_custom_call" | custom-call | tf_op jit(solution)/shard_map/last/pallas_call | solution.py:1335

commit v3 on v2

--- a/solution.py
+++ b/solution.py
@@ -792,7 +792,7 @@
     columns = [slice(m * width, (m + 1) * width) for m in range(3)]
     g_qkv = [Gather(place, s_qkv.at[:, columns[m]], f_qkv.at[:, columns[m]], 128 if m == 2 else 256, q_send.at[m], q_recv.at[m]) for m in range(3)]
     g_out = Gather(place, s_out, f_out, 256, q_send.at[3], q_recv.at[3])
-    g_ups = [Gather(place, s_up3.at[t], f_up.at[t], (256, 384, 256)[t], m_send.at[t], m_recv.at[t]) for t in range(3)]
+    g_ups = [Gather(place, s_up3.at[t], f_up.at[t], (256, 256, 256)[t], m_send.at[t], m_recv.at[t]) for t in range(3)]
     g_downs = [Gather(place, s_down.at[t * 128 : t * 128 + 128], f_down.at[t], 256, m_send.at[3 + t], m_recv.at[3 + t]) for t in range(3)]
     groups = {"q": g_qkv[:1], "k": g_qkv[1:2], "v": g_qkv[2:], "o": [g_out]}
     groups.update({f"p{t}": [g_ups[t], g_downs[t]] for t in range(3)})
@@ -925,9 +925,9 @@
         if part and t < 2:
             swaps["up", t].start()
             swaps["down", t].start()
-        elif part:
-            later.start("g_up2", lambda: g_up.at[0], h_gup)
-            later.start("g_down2", lambda: g_down.at[0], h_gdown)
+        elif t == 2:
+            later.start(f"g_up2{part}", lambda: g_up.at[0, :, :, :, part], lambda: h_gup.at[:, :, :, part])
+            later.start(f"g_down2{part}", lambda: g_down.at[0, 2 * part : 2 * part + 2], lambda: h_gdown.at[2 * part : 2 * part + 2])
 
     def feed(step, _):
         t, c = step // 4, step % 4
@@ -1292,7 +1292,7 @@
             + [pltpu.SemaphoreType.DMA((4, 28))] * 2
             + [pltpu.SemaphoreType.DMA((6, 28))] * 2
             + [pltpu.SemaphoreType.DMA((7,))] * 2
-            + [pltpu.SemaphoreType.DMA((12,)), pltpu.SemaphoreType.DMA((33,)), pltpu.SemaphoreType.DMA((2,))]
+            + [pltpu.SemaphoreType.DMA((12,)), pltpu.SemaphoreType.DMA((35,)), pltpu.SemaphoreType.DMA((2,))]
             + [pltpu.SemaphoreType.DMA((4,))] * 2
             + [pltpu.SemaphoreType.DMA((2, 10))] * 2,
             compiler_params=pltpu.CompilerParams(vmem_limit_bytes=LIMIT, collective_id=0, has_side_effects=True),

time: 188 us -> 187 us (level)
  no operation moved by 1% of the time
where the time goes in v3:
time: 187 us
  Pallas kernels  186 us (99%)
    pallas_call x1, Pallas kernels, shards(): pl.pallas_call(functools.partial(first_kernel, images, slots, width), out...  101 us
    pallas_call x1, Pallas kernels, shards(): pl.pallas_call(functools.partial(second_kernel, images, slots, width), ou...  77.8 us
    pallas_call x1, Pallas kernels, shards(): pl.pallas_call(functools.partial(last_kernel, images, width), out_shape=[...  7.53 us

profile of v3, /device:TPU:1, one launch (start us, length us, event | category | flops | bytes accessed | tf_op | source)
XLA Modules:
  0.0 187.1 jit_solution(6268316577175838580)
XLA Ops:
  0.7 100.8 %first.1 = (f32[16,768]{1,0:T(8,128)}, f32[3,1,1024]{2,1,0:T(1,128)}, bf16[1024,768]{1,0:T(8,128)(2,1)}, bf16[768,1024]{1,0:T(8,128)(2,1)}, bf16[1024,768]{1,0:T...) custom-call(bf16[5,197,768]{2,1,0:T(8,128)(2,1)} %h_patches.1, ...), custom_call_target="tpu_custom_call" | custom-call | tf_op jit(solution)/shard_map/first/pallas_call | solution.py:1286
  101.5 77.8 %second.1 = (f32[5,197,768]{2,1,0:T(8,128)}, bf16[5,197,768]{2,1,0:T(8,128)(2,1)}, bf16[96,6144]{1,0:T(8,128)(2,1)}, bf16[384,768]{1,0:T(8,128)(2,1)}, f32[16,128]{1,0:T(8,128)}) custom-call(s32[5,197]{1,0:T(8,128)} %keep_in.3, f32[16,768]{1,0:T(8,128)} %get-tuple-element.57.vectors, f32[3,1,1024]{2,1,0:T(1,128)} %get-tuple-element.58.s_bup, ...), custom_call_target="tpu_custom_call" | custom-call | tf_op jit(solution)/shard_map/second/pallas_call | solution.py:1319
  179.3 7.5 %last.1 = (f32[5,197,768]{2,1,0:T(8,128)}, bf16[5,197,768]{2,1,0:T(8,128)(2,1)}, f32[96,2304]{1,0:T(8,128)}, f32[96,3072]{1,0:T(8,128)}, f32[96,768]{1,0:T(8,128...) custom-call(f32[5,197,768]{2,1,0:T(8,128)} %get-tuple-element.79.h_p, ...), custom_call_target="tpu_custom_call" | custom-call | tf_op jit(solution)/shard_map/last/pallas_call | solution.py:1335
